TPU v7x, 512 devices: a whole 4x4x16 slice. The times are simulated.
512 devices in a mesh: wide: 64 (over x, z_hi, y, core), narrow: 8 (over z_lo).
Axes of the slice: x: 4, y: 4, z: 16 (z_hi: 2, z_lo: 8; z = z_hi * 8 + z_lo), core: 2. Of those that a mesh axis runs over, the one named last changes fastest.
Arguments:
- pair_rep: bfloat16 [512, 512, 128], P('wide', 'narrow'), may hold values from -6 to 6
- pair_gain: float32 [128], replicated, may hold values from 0.1 to 1.9
- pair_bias: float32 [128], replicated, may hold values from -3 to 3
- left_weight: bfloat16 [128, 256], replicated, may hold values from -0.5 to 0.5
- right_weight: bfloat16 [128, 256], replicated, may hold values from -0.5 to 0.5
- gate_weight: bfloat16 [128, 128], replicated, may hold values from -0.5 to 0.5
- out_weight: bfloat16 [128, 128], replicated, may hold values from -0.5 to 0.5
- out_gain: float32 [128], replicated, may hold values from 0.1 to 1.9
- out_bias: float32 [128], replicated, may hold values from -3 to 3
Outputs:
- update_t: bfloat16 [512, 128, 512], P('wide', 'narrow')
All inputs are finite; a program needn't handle non-finite values.
Results may differ from a plain program's by a relative error of at most 0.0053.
Values may be sent and summed in bfloat16 or wider, within the bound.
No kernel may reach another device: no remote copies, remote signals or barrier semaphores. Data moves between devices by JAX's collectives and lax.ppermute only.
A program may use at most 64 MiB of HBM per device.

v0:
```python
import jax
import jax.numpy as jnp
from jax import lax
from jax.sharding import PartitionSpec as P


def layer_norm(values, gain, bias):
    center = jnp.mean(values, axis=-1, keepdims=True)
    spread = jnp.mean((values - center) ** 2, axis=-1, keepdims=True)
    return (values - center) * lax.rsqrt(spread + 1e-05) * gain + bias


def gated_pair(projected, width):
    left_edge = (jax.nn.sigmoid(projected[width : 2 * width]) * projected[:width]).astype(
        jnp.bfloat16
    )
    right_edge = (jax.nn.sigmoid(projected[3 * width :]) * projected[2 * width : 3 * width]).astype(
        jnp.bfloat16
    )
    return (left_edge, right_edge)


def shards(
    pair_rep,
    pair_gain,
    pair_bias,
    left_weight,
    right_weight,
    gate_weight,
    out_weight,
    out_gain,
    out_bias,
):
    hidden = out_weight.shape[0]
    parts = lax.axis_size("narrow")
    share = hidden // parts
    offset = lax.axis_index("narrow") * share
    pair_normed = layer_norm(pair_rep.astype(jnp.float32), pair_gain, pair_bias).astype(
        jnp.bfloat16
    )
    all_columns = jnp.concatenate([left_weight, right_weight], axis=1)
    projected = jnp.einsum(
        "ikc,cg->gik", pair_normed, all_columns, preferred_element_type=jnp.float32
    )
    left_edge, right_edge = gated_pair(projected, hidden)
    left_edge, right_edge = (
        lax.all_to_all(left_edge, "narrow", split_axis=0, concat_axis=2, tiled=True),
        lax.all_to_all(right_edge, "narrow", split_axis=0, concat_axis=2, tiled=True),
    )
    triangle = jnp.einsum(
        "hik,hjk->hij",
        left_edge,
        lax.all_gather(right_edge, "wide", axis=1, tiled=True),
        preferred_element_type=jnp.float32,
    )
    sums, squares = lax.psum(
        (jnp.sum(triangle, axis=0), jnp.sum(triangle * triangle, axis=0)), "narrow"
    )
    center = sums / hidden
    spread = squares / hidden - center * center
    own_gain = lax.dynamic_slice_in_dim(out_gain, offset, share, 0)
    own_bias = lax.dynamic_slice_in_dim(out_bias, offset, share, 0)
    tri_normed = (triangle - center) * lax.rsqrt(spread + 1e-05)
    tri_normed = (tri_normed * own_gain[:, None, None] + own_bias[:, None, None]).astype(
        jnp.bfloat16
    )
    own_weight = lax.dynamic_slice_in_dim(out_weight, offset, share, 0)
    projected_out = lax.psum_scatter(
        jnp.einsum("hij,hc->jic", tri_normed, own_weight, preferred_element_type=jnp.float32),
        "narrow",
        scatter_dimension=0,
        tiled=True,
    )
    out_gate = jax.nn.sigmoid(
        jnp.einsum("ijc,cd->jid", pair_normed, gate_weight, preferred_element_type=jnp.float32)
    )
    update = (out_gate * projected_out).astype(jnp.bfloat16)
    moved = lax.all_to_all(
        lax.all_to_all(update, "narrow", split_axis=2, concat_axis=0, tiled=True),
        "wide",
        split_axis=0,
        concat_axis=1,
        tiled=True,
    )
    return jnp.transpose(moved, (0, 2, 1))


def solution(mesh):
    in_specs = (P("wide", "narrow", None), P(), P(), P(), P(), P(), P(), P(), P())
    out_specs = P("wide", "narrow", None)
    return jax.shard_map(shards, mesh=mesh, in_specs=in_specs, out_specs=out_specs, check_vma=False)
```

profile of v0, /device:TPU:1, one launch (start us, length us, event | category | flops | bytes accessed | tf_op | source)
XLA Modules:
  0.0 402.4 jit_solution(2217745906155521440)
XLA Ops:
  6.5 0.0 copy-start
  6.5 0.0 all-gather.2.cloned.1.call-start
  6.5 1.1 convert_reduce_fusion
  7.6 1.2 fusion.8
  8.8 1.3 fusion.20
  10.1 0.1 fusion.12
  10.3 0.2 copy.27
  10.5 0.2 reshape.23
  10.7 23.2 %all_to_all.72 = bf16[8,2,4096]{2,1,0:T(2,128)(2,1)S(1)} all-to-all(bf16[8,2,4096]{2,1,0:T(2,128)(2,1)S(1)} %reshape.23), channel_id=1, replica_groups=mesh['wide'=64,'narrow'=8] {'narrow'}, dimensions={0} | all-to-all | bytes 262144 | tf_op jit(solution)/shard_map/all_to_all | solution.py:48
  33.9 0.2 reshape.24
  34.2 0.2 copy.28
  34.3 0.0 copy-start.1
  34.4 0.0 copy-start.2
  34.4 0.0 copy-start.3
  34.4 0.0 copy-start.4
  34.4 0.9 all_to_all.59
  35.3 0.0 all-gather.2.cloned.1.call-update
  35.3 0.2 copy.25
  35.5 0.9 reshape.21
  36.4 5.6 %all-to-all-start = ((bf16[8,2,4096]{2,1,0:T(2,128)(2,1)}), bf16[8,2,4096]{2,1,0:T(2,128)(2,1)S(1)}, u32[]{:S(2)}, u32[]{:S(2)}) async-start(bf16[8,2,4096]{2,1,0:T(2,128)(2,1)} %reshape.21), calls=%async_computation | async-start | bytes 262144 | tf_op jit(solution)/shard_map/all_to_all | solution.py:47
  42.0 0.0 reduce-scatter.2.cloned.1.call-start
  42.0 0.7 dynamic_slice.11
  42.8 0.7 dynamic_slice.10
  43.5 8.8 %all-to-all-done = bf16[8,2,4096]{2,1,0:T(2,128)(2,1)S(1)} async-done(((bf16[8,2,4096]{2,1,0:T(2,128)(2,1)}), bf16[8,2,4096]{2,1,0:T(2,128)(2,1)S(1)}, u32[]{:S(2)}, u32[]{:S(2)}) %all-to-all-start) | async-done | bytes 131104 | tf_op jit(solution)/shard_map/all_to_all | solution.py:47
  52.3 0.2 reshape.22
  52.5 0.2 copy.26
  52.7 0.2 all_to_all.55
  52.9 164.2 %all-gather.2.cloned.1.call-done = bf16[16,512,512]{2,1,0:T(8,128)(2,1)} async-done(((bf16[16,8,512]{2,1,0:T(8,128)(2,1)}), bf16[16,512,512]{2,1,0:T(8,128)(2,1)}) %all-gather.2.cloned.1.call-update) | async-done | bytes 8388624 | tf_op jit(solution)/shard_map/all_gather | solution.py:53
  217.1 5.6 %fusion.31 = (f32[8,512]{1,0:T(8,128)S(1)}, f32[8,512]{1,0:T(8,128)S(1)}, f32[16,8,512]{2,1,0:T(8,128)S(1)}) fusion(bf16[16,8,512]{2,1,0:T(8,128)(2,1)S(1)} %all_to_all.55, bf16[16,512,512]{2,1,0:T(8,128)(2,1)} %all-gather.2.cloned.1.call-done), kind=kOutput, calls=%fused_computation.45 | convolution fusion | flops 67297280 | bytes 8814592 | tf_op jit(solution)/shard_map/hik,hjk->hij/dot_general | solution.py:50
  222.7 41.9 %all-reduce = (f32[8,512]{1,0:T(8,128)S(1)}, f32[8,512]{1,0:T(8,128)S(1)}) all-reduce(f32[8,512]{1,0:T(8,128)S(1)} %get-tuple-element.6, f32[8,512]{1,0:T(8,128)S(1)} %get-tuple-element.5), channel_id=1, replica_groups=mesh['wide'=64,'narrow'=8] {'narrow'}, use_global_device_ids=true, to_apply=%region_5.0 | all-reduce | flops 8192 | bytes 65536 | tf_op jit(solution)/shard_map/psum | solution.py:56
  264.6 0.1 add_convert_fusion
  264.7 0.0 copy-done
  264.7 1.9 convolution_bitcast_fusion
  266.6 0.0 reduce-scatter.2.cloned.1.call-update
  266.7 70.5 %reduce-scatter.2.cloned.1.call-done = f32[64,8,128]{2,0,1:T(8,128)} async-done(((f32[512,8,128]{2,0,1:T(8,128)}), f32[64,8,128]{2,0,1:T(8,128)}) %reduce-scatter.2.cloned.1.call-update) | async-done | bytes 262160 | tf_op jit(solution)/shard_map/reduce_scatter | solution.py:68
  337.2 0.0 copy-done.1
  337.2 0.0 copy-done.2
  337.2 1.3 fusion.5
  338.5 0.2 copy.31
  338.7 0.2 reshape.25
  338.9 15.5 %all_to_all.73 = bf16[8,2,4096]{2,1,0:T(2,128)(2,1)S(1)} all-to-all(bf16[8,2,4096]{2,1,0:T(2,128)(2,1)S(1)} %reshape.25), channel_id=1, replica_groups=mesh['wide'=64,'narrow'=8] {'narrow'}, dimensions={0} | all-to-all | bytes 262144 | tf_op jit(solution)/shard_map/all_to_all | solution.py:79
  354.5 0.2 reshape.26
  354.7 0.6 copy.39
  355.3 1.1 reshape.27
  356.4 37.2 %all_to_all.74 = bf16[64,2,512]{2,1,0:T(2,128)(2,1)S(1)} all-to-all(bf16[64,2,512]{2,1,0:T(2,128)(2,1)S(1)} %reshape.27), channel_id=1, replica_groups=mesh['wide'=64,'narrow'=8] {'wide'}, dimensions={0} | all-to-all | bytes 262144 | tf_op jit(solution)/shard_map/all_to_all | solution.py:78
  393.7 0.7 reshape.28
  394.4 0.2 copy.44
  394.6 1.0 copy.36
  (5 shorter events, 0.0 us)
Async XLA Ops:
  6.5 258.2 %copy-start = (bf16[128,128]{1,0:T(8,128)(2,1)S(1)}, bf16[128,128]{1,0:T(8,128)(2,1)}, u32[]{:S(2)}) copy-start(bf16[128,128]{1,0:T(8,128)(2,1)} %param.15) | copy-start | bytes 98308
  6.5 210.5 %all-gather.2.cloned.1.call-start = ((), (), s32[]{:S(2)}) async-start(), calls=%async_computation.5 | async-start | bytes 8519680 | tf_op jit(solution)/shard_map/all_gather | solution.py:53
  34.3 302.9 %copy-start.1 = (bf16[8,64,128]{2,1,0:T(8,128)(2,1)S(1)}, bf16[8,64,128]{2,1,0:T(8,128)(2,1)}, u32[]{:S(2)}) copy-start(bf16[8,64,128]{2,1,0:T(8,128)(2,1)} %param.9) | copy-start | bytes 393220
  34.4 302.8 %copy-start.2 = (f32[128]{0:T(128)S(1)}, f32[128]{0:T(128)}, u32[]{:S(2)}) copy-start(f32[128]{0:T(128)} %param.11) | copy-start | bytes 1540
  34.4 302.8 %copy-start.3 = (f32[128]{0:T(128)S(1)}, f32[128]{0:T(128)}, u32[]{:S(2)}) copy-start(f32[128]{0:T(128)} %param.10) | copy-start | bytes 1540
  34.4 302.8 %copy-start.4 = (bf16[128,128]{1,0:T(8,128)(2,1)S(1)}, bf16[128,128]{1,0:T(8,128)(2,1)}, u32[]{:S(2)}) copy-start(bf16[128,128]{1,0:T(8,128)(2,1)} %param.14) | copy-start | bytes 98308
  36.4 15.9 %all-to-all-start = ((bf16[8,2,4096]{2,1,0:T(2,128)(2,1)}), bf16[8,2,4096]{2,1,0:T(2,128)(2,1)S(1)}, u32[]{:S(2)}, u32[]{:S(2)}) async-start(bf16[8,2,4096]{2,1,0:T(2,128)(2,1)} %reshape.21), calls=%async_computation | async-start | bytes 262144 | tf_op jit(solution)/shard_map/all_to_all | solution.py:47
  42.0 295.2 %reduce-scatter.2.cloned.1.call-start = ((), (), s32[]{:S(2)}) async-start(), calls=%async_computation.6 | async-start | bytes 2359296 | tf_op jit(solution)/shard_map/reduce_scatter | solution.py:68
Sparse Core Ops, SparseCore 0:
  35.4 181.6 all-gather.1
  266.8 70.3 reduce-scatter.1
where the time goes:
time: 404 us; the launch traced here: 402 us
  waiting for transfers between devices  244 us (60%)
  blocking collectives  118 us (29%)
  between operations  13.6 us (3%)
  matrix products  10.2 us (3%)
  local copies, waits for them, and re-layouts  9.1 us (2%)
  starting transfers between devices  5.66 us (1%)
    all_gather x1, waiting for transfers between devices, shards(): lax.all_gather(right_edge, 'wide', axis=1, tiled=True)  164 us
    reduce_scatter x1, waiting for transfers between devices, shards(): lax.psum_scatter(jnp.einsum('hij,hc->jic', tri_normed, own_weight, prefer...  70.5 us
    psum x1, blocking collectives, shards(): lax.psum((jnp.sum(triangle, axis=0), jnp.sum(triangle * triangle, axis=0)...  41.9 us
    all_to_all x1, blocking collectives, shards(): lax.all_to_all(lax.all_to_all(update, 'narrow', split_axis=2, concat_axis...  37.2 us
    all_to_all x1, blocking collectives, shards(): lax.all_to_all(right_edge, 'narrow', split_axis=0, concat_axis=2, tiled=T...  23.2 us
    all_to_all x1, blocking collectives, shards(): lax.all_to_all(update, 'narrow', split_axis=2, concat_axis=0, tiled=True)  15.5 us
    all_to_all x1, waiting for transfers between devices, shards(): lax.all_to_all(left_edge, 'narrow', split_axis=0, concat_axis=2, tiled=True)  8.79 us
  transfers between devices with their start and end apart: 3, of which 3 were waited for; matrix products, arithmetic and copies ran while one was open for 1% of the time, Pallas kernels for 0%

commit v1 on v0

v1 whole, which is shorter than its diff:
```python
import jax
import jax.numpy as jnp
import numpy as np
from jax import lax
from jax.experimental import pallas as pl
from jax.experimental.pallas import tpu as pltpu
from jax.sharding import Mesh, PartitionSpec as P

F32 = jnp.float32
BF16 = jnp.bfloat16
ROWS = 8
SPLIT = ("n", "zh", "y")


def params():
    return pltpu.CompilerParams(vmem_limit_bytes=48 * 1024 * 1024)


def lane_mask(shape):
    return lax.broadcasted_iota(jnp.int32, shape, len(shape) - 1) < 64


def swap_halves(values):
    return pltpu.roll(values, 64, len(values.shape) - 1)


def edges_kernel(pair, gain, bias, left_weight, right_weight, edges, normed, scratch, gate_rows):
    values = pair[...].astype(F32).reshape(512, 128)
    center = jnp.mean(values, axis=-1, keepdims=True)
    moved = values - center
    spread = jnp.mean(moved * moved, axis=-1, keepdims=True)
    scaled = moved * lax.rsqrt(spread + 1e-05) * gain[...] + bias[...]
    rounded = scaled.astype(BF16)
    for row in range(ROWS):
        gate_rows[pl.ds(row, 64, stride=ROWS), :] = scaled[row * 64 : row * 64 + 64]
    normed[...] = gate_rows[...].astype(BF16)
    for side, weight in enumerate((left_weight, right_weight)):
        both = lax.dot_general(
            weight[...], rounded, (((0,), (1,)), ((), ())), preferred_element_type=F32
        )
        edge = jax.nn.sigmoid(both[128:]) * both[:128]
        for pair_of_rows in range(4):
            lanes = slice(pair_of_rows * 128, pair_of_rows * 128 + 128)
            first, second = edge[:64, lanes], edge[64:, lanes]
            low = lane_mask(first.shape)
            even = jnp.where(low, first, swap_halves(second))
            odd = jnp.where(low, swap_halves(first), second)
            start = side * 8 + pair_of_rows * 2
            scratch[pl.ds(start, 64, stride=16), :] = even
            scratch[pl.ds(start + 1, 64, stride=16), :] = odd
    edges[...] = scratch[...].astype(BF16)


def make_edges(pair, gain, bias, left_weight, right_weight):
    return pl.pallas_call(
        edges_kernel,
        out_shape=(
            jax.ShapeDtypeStruct((1024, 128), BF16),
            jax.ShapeDtypeStruct((512, 128), BF16),
        ),
        scratch_shapes=[pltpu.VMEM((1024, 128), F32), pltpu.VMEM((512, 128), F32)],
        compiler_params=params(),
        name="edges",
    )(pair, gain.reshape(1, 128), bias.reshape(1, 128), left_weight, right_weight)


def triangle_kernel(core, own, other, edges, out):
    first_core = core[0] == 0
    total = jnp.zeros((128, 512), F32)
    for part in range(8):
        mine = own[:, part].astype(F32).reshape(32, 8, 128)
        theirs = other[:, part].astype(F32).reshape(32, 8, 128)
        rows = jnp.concatenate(
            [jnp.where(first_core, mine, theirs), jnp.where(first_core, theirs, mine)], axis=1
        )
        left = rows.reshape(512, 128).astype(BF16)
        right = edges[part].astype(F32)[:, 8:].reshape(64, 128)
        low = lane_mask(right.shape)
        right = jnp.concatenate(
            [jnp.where(low, right, 0.0), jnp.where(low, 0.0, right)], axis=0
        ).astype(BF16)
        total += lax.dot_general(
            right, left, (((1,), (1,)), ((), ())), preferred_element_type=F32
        )
    shape = (64, 128)
    low = lane_mask(shape)
    upper = lax.broadcasted_iota(jnp.int32, shape, 0) % 8 < 4
    for block in range(4):
        columns = total[:, block * 128 : block * 128 + 128]
        turned = []
        for hidden in range(2):
            held = columns[hidden * 64 : hidden * 64 + 64]
            up, down = pltpu.roll(held, 60, 0), pltpu.roll(held, 4, 0)
            crossed = swap_halves(jnp.where(upper, up, down))
            turned.append(jnp.where(upper == low, held, crossed))
        even = jnp.where(upper, turned[0], pltpu.roll(turned[1], 4, 0))
        odd = jnp.where(upper, pltpu.roll(turned[0], 60, 0), turned[1])
        out[block * 2] = even.astype(BF16)
        out[block * 2 + 1] = odd.astype(BF16)


def make_triangle(core, own, other, edges):
    return pl.pallas_call(
        triangle_kernel,
        out_shape=jax.ShapeDtypeStruct((8, 64, 128), BF16),
        in_specs=[pl.BlockSpec(memory_space=pltpu.SMEM)]
        + [pl.BlockSpec(memory_space=pltpu.VMEM)] * 3,
        compiler_params=params(),
        name="triangle",
    )(core, own, other, edges)


def update_kernel(triangle, normed, gate_weight, out_weight, gain, bias, out, scratch):
    values = triangle[...].astype(F32)
    sums = jnp.sum(values, axis=0)
    squares = jnp.sum(values * values, axis=0)
    center = (sums + pltpu.roll(sums, 4, 0)) / 128
    spread = (squares + pltpu.roll(squares, 4, 0)) / 128 - center * center
    scale = lax.rsqrt(spread + 1e-05)
    scratch[...] = ((values - center) * scale).reshape(512, 128)
    tall_gain = jnp.transpose(jnp.broadcast_to(gain[...], (128, 128)))
    tall_bias = jnp.transpose(jnp.broadcast_to(bias[...], (128, 128)))
    for part in range(4):
        held = jnp.concatenate(
            [
                scratch[pl.ds(part, 64, stride=8), :],
                scratch[pl.ds(4 + part, 64, stride=8), :],
            ],
            axis=0,
        )
        held = (held * tall_gain + tall_bias).astype(BF16)
        projected = lax.dot_general(
            out_weight[...], held, (((0,), (0,)), ((), ())), preferred_element_type=F32
        )
        rows = jnp.concatenate(
            [
                normed[:, part].astype(F32).reshape(64, 128),
                normed[:, 4 + part].astype(F32).reshape(64, 128),
            ],
            axis=0,
        ).astype(BF16)
        logits = lax.dot_general(
            gate_weight[...], rows, (((0,), (1,)), ((), ())), preferred_element_type=F32
        )
        update = (jax.nn.sigmoid(logits) * projected).astype(BF16)
        out[:, part] = update.reshape(8, 16, 128)


def make_update(triangle, normed, gate_weight, out_weight, gain, bias):
    return pl.pallas_call(
        update_kernel,
        out_shape=jax.ShapeDtypeStruct((8, 4, 16, 128), BF16),
        scratch_shapes=[pltpu.VMEM((512, 128), F32)],
        compiler_params=params(),
        name="update",
    )(triangle, normed, gate_weight, out_weight, gain.reshape(1, 128), bias.reshape(1, 128))


def order_kernel(update, out):
    for block in range(4):
        first = update[block * 2].astype(F32).reshape(64, 128)
        second = update[block * 2 + 1].astype(F32).reshape(64, 128)
        low = lane_mask(first.shape)
        upper = jnp.where(low, first, swap_halves(second)).astype(BF16)
        lower = jnp.where(low, swap_halves(first), second).astype(BF16)
        lanes = slice(block * 128, block * 128 + 128)
        out[:4, :, lanes] = upper.reshape(4, 16, 128)
        out[4:, :, lanes] = lower.reshape(4, 16, 128)


def make_order(update):
    return pl.pallas_call(
        order_kernel,
        out_shape=jax.ShapeDtypeStruct((8, 16, 512), BF16),
        compiler_params=params(),
        name="order",
    )(update)


def exchange(values, axes):
    return lax.all_to_all(values, axes, 0, 0, tiled=True)


def shards(
    pair_rep,
    pair_gain,
    pair_bias,
    left_weight,
    right_weight,
    gate_weight,
    out_weight,
    out_gain,
    out_bias,
):
    edges, normed = make_edges(pair_rep, pair_gain, pair_bias, left_weight, right_weight)
    swapped = [((a * 8 + e) * 8 + n, (n * 8 + e) * 8 + a) for a in range(8) for e in range(8) for n in range(8)]
    normed = exchange(normed.reshape(8, 8, 8, 128), ("y", "co"))
    normed = lax.ppermute(normed, ("x", "zh", "y", "co", "n"), swapped)
    edges = exchange(edges.reshape(64, 16, 128), SPLIT).reshape(8, 8, 16, 128)
    left = edges[:, :, :8]
    own = exchange(jnp.broadcast_to(left[None], (4,) + left.shape), "x")
    other = lax.ppermute(own, "co", [(0, 1), (1, 0)])
    core = lax.axis_index("co").astype(jnp.int32).reshape(1)
    triangle = make_triangle(core, own, other, edges)
    triangle = exchange(triangle.reshape(64, 8, 128), SPLIT)
    update = make_update(triangle, normed, gate_weight, out_weight, out_gain, out_bias)
    return make_order(exchange(update, "n"))


def solution(mesh):
    fine = Mesh(mesh.devices.reshape(4, 2, 4, 2, 8), ("x", "zh", "y", "co", "n"))
    rows = ("x", "zh", "y", "co")
    in_specs = (P(rows, "n", None), P(), P(), P(), P(), P(), P(), P(), P())
    out_specs = P(rows, "n", None)
    return jax.shard_map(shards, mesh=fine, in_specs=in_specs, out_specs=out_specs, check_vma=False)
```

time: 404 us -> 118 us (0.29)
  waiting for transfers between devices: 244 us -> 18.2 us
  blocking collectives: 118 us -> 74.2 us
  between operations: 13.6 us -> 0.09 us
  starting transfers between devices: 5.66 us -> 16.5 us
  matrix products: 10.2 us -> 0 us
  local copies, waits for them, and re-layouts: 9.1 us -> 4.05 us
    all_gather x1 -> x0, waiting for transfers between devices: 164 us -> none  [shards(): lax.all_gather(right_edge, 'wide', axis=1, tiled=True)]
    reduce_scatter x1 -> x0, waiting for transfers between devices: 70.5 us -> none  [shards(): lax.psum_scatter(jnp.einsum('hij,hc->jic', tri_normed, own_weight, prefer...]
    psum x1 -> x0, blocking collectives: 41.9 us -> none  [shards(): lax.psum((jnp.sum(triangle, axis=0), jnp.sum(triangle * triangle, axis=0)...]
    dot_general x4 -> x0, matrix products: 10.2 us -> none  [the longest x1 5.65 us: shards(): jnp.einsum('hik,hjk->hij', left_edge, lax.all_gather(right_edge, 'wide',...]
    all_to_all x1 -> x2, waiting for transfers between devices: 8.79 us -> 18.2 us  [exchange(): return lax.all_to_all(values, axes, 0, 0, tiled=True)]
    ppermute x0 -> x2, starting transfers between devices: none -> 7.2 us  [the longest x1 6.53 us: shards(): other = lax.ppermute(own, 'co', [(0, 1), (1, 0)])]
    all_to_all x1 -> x2, starting transfers between devices: 5.62 us -> 9.35 us  [exchange(): return lax.all_to_all(values, axes, 0, 0, tiled=True)]
  transfers between devices with their start and end apart: 3 -> 4, of which waited for: 3 -> 2; matrix products, arithmetic and copies ran while one was open for 1% -> 0% of each run, Pallas kernels for 0% -> 1%
where the time goes in v1:
time: 118 us; the launch traced here: 116 us
  blocking collectives  74.2 us (63%)
  waiting for transfers between devices  18.2 us (15%)
  starting transfers between devices  16.5 us (14%)
  local copies, waits for them, and re-layouts  4.05 us (3%)
  Pallas kernels  3.29 us (3%)
    all_to_all x3, blocking collectives, exchange(): return lax.all_to_all(values, axes, 0, 0, tiled=True)  74.2 us
    all_to_all x2, waiting for transfers between devices, exchange(): return lax.all_to_all(values, axes, 0, 0, tiled=True)  18.2 us
    all_to_all x2, starting transfers between devices, exchange(): return lax.all_to_all(values, axes, 0, 0, tiled=True)  9.35 us
    ppermute x1, starting transfers between devices, shards(): other = lax.ppermute(own, 'co', [(0, 1), (1, 0)])  6.53 us
    unnamed x18, local copies, waits for them, and re-layouts  3.92 us
  transfers between devices with their start and end apart: 4, of which 2 were waited for; matrix products, arithmetic and copies ran while one was open for 0% of the time, Pallas kernels for 1%

profile of v1, /device:TPU:1, one launch (start us, length us, event | category | flops | bytes accessed | tf_op | source)
XLA Modules:
  0.0 116.4 jit_solution(11087891171325769565)
XLA Ops:
  0.0 0.0 copy-start.5
  0.0 0.0 copy-start.6
  0.0 0.7 copy-done.5
  0.7 0.0 copy-done.6
  0.7 0.0 copy-start
  0.7 0.9 copy-done
  1.6 0.0 copy-start.1
  1.6 0.8 copy-done.1
  2.4 0.0 copy-start.2
  2.4 0.8 copy-done.2
  3.3 0.9 edges.1
  4.2 38.7 %all_to_all.25 = bf16[64,16,128]{2,1,0:T(8,128)(2,1)S(1)} all-to-all(bf16[64,16,128]{2,1,0:T(8,128)(2,1)S(1)} %bitcast.11), channel_id=1, replica_groups=mesh['x'=4,'zh'=2,'y'=4,'co'=2,'n'=8] {'n','zh','y'}, dimensions={0} | all-to-all | bytes 524288 | tf_op jit(solution)/shard_map/all_to_all | solution.py:181
  42.9 0.1 broadcast_in_dim.2
  43.1 10.7 %all_to_all.26.own = bf16[4,8,8,8,128]{4,3,2,1,0:T(8,128)(2,1)S(1)} all-to-all(bf16[4,8,8,8,128]{4,3,2,1,0:T(8,128)(2,1)S(1)} %broadcast_in_dim.2), channel_id=1, replica_groups=mesh['x'=4,'zh'=2,'y'=4,'co'=2,'n'=8] {'x'}, dimensions={0} | all-to-all | bytes 1048576 | tf_op jit(solution)/shard_map/all_to_all | solution.py:181
  53.8 6.5 %collective-permute-start = (bf16[4,8,8,8,128]{4,3,2,1,0:T(8,128)(2,1)S(1)}, bf16[4,8,8,8,128]{4,3,2,1,0:T(8,128)(2,1)S(1)}, u32[]{:S(2)}, u32[]{:S(2)}) collective-permute-start(bf16[4,8,8,8,128]{4,3,2,1,0:T(8,128)(2,1)S(1)} %all_to_all.26.own), channel_id=1, source_target_pairs={{0,8},{8,0},{1,9},{9,1},{2,10},{10,2},{3,11},{11,3},{4,12},{12,4},... | collective-permute-start | bytes 1572872 | tf_op jit(solution)/shard_map/ppermute | solution.py:202
  60.3 3.3 %all-to-all-start.3 = ((bf16[8,8,8,128]{3,2,1,0:T(8,128)(2,1)}), bf16[8,8,8,128]{3,2,1,0:T(8,128)(2,1)S(1)}, u32[]{:S(2)}, u32[]{:S(2)}) async-start(bf16[8,8,8,128]{3,2,1,0:T(8,128)(2,1)} %bitcast.6), calls=%async_computation.3 | async-start | bytes 262144 | tf_op jit(solution)/shard_map/all_to_all | solution.py:181
  63.7 0.0 collective-permute-done.other
  63.7 1.2 %triangle.1 = bf16[8,64,128]{2,1,0:T(8,128)(2,1)} custom-call(s32[1]{0:T(128)} %bitcast.core, bf16[4,8,8,8,128]{4,3,2,1,0:T(8,128)(2,1)S(1)} %all_to_all.26.own, bf16[4,8,8,8,128]{4,3,2,1,0:T(8,128)(2,1)S(1)} %collective-permute-done.other, bf16[8,8,16,128]{3,2,1,0:T(8,128)(2,1)S(1)} %bitcast.10), custom_call_target="tpu_custom_call" | custom-call | tf_op jit(solution)/shard_map/triangle/pallas_call | solution.py:103
  64.9 4.0 %all-to-all-done.3 = bf16[8,8,8,128]{3,2,1,0:T(8,128)(2,1)S(1)} async-done(((bf16[8,8,8,128]{3,2,1,0:T(8,128)(2,1)}), bf16[8,8,8,128]{3,2,1,0:T(8,128)(2,1)S(1)}, u32[]{:S(2)}, u32[]{:S(2)}) %all-to-all-start.3) | async-done | bytes 131104 | tf_op jit(solution)/shard_map/all_to_all | solution.py:181
  68.9 0.0 copy-start.3
  68.9 0.0 copy-start.4
  68.9 6.0 %all-to-all-start.2 = ((bf16[64,8,128]{2,1,0:T(8,128)(2,1)}), bf16[64,8,128]{2,1,0:T(8,128)(2,1)S(1)}, u32[]{:S(2)}, u32[]{:S(2)}) async-start(bf16[64,8,128]{2,1,0:T(8,128)(2,1)} %bitcast.5), calls=%async_computation.2 | async-start | bytes 262144 | tf_op jit(solution)/shard_map/all_to_all | solution.py:181
  75.0 0.7 collective-permute-start.1
  75.6 0.0 collective-permute-done.1.normed
  75.6 14.2 %all-to-all-done.2.triangle = bf16[64,8,128]{2,1,0:T(8,128)(2,1)S(1)} async-done(((bf16[64,8,128]{2,1,0:T(8,128)(2,1)}), bf16[64,8,128]{2,1,0:T(8,128)(2,1)S(1)}, u32[]{:S(2)}, u32[]{:S(2)}) %all-to-all-start.2) | async-done | bytes 131104 | tf_op jit(solution)/shard_map/all_to_all | solution.py:181
  89.9 0.0 copy-start.7
  89.9 0.0 copy-start.8
  89.9 0.0 copy-done.3
  89.9 0.0 copy-done.4
  89.9 0.6 copy-done.7
  90.5 0.0 copy-done.8
  90.5 0.4 update.1
  90.9 24.7 %all_to_all.27.update = bf16[8,4,16,128]{3,2,1,0:T(8,128)(2,1)S(1)} all-to-all(bf16[8,4,16,128]{3,2,1,0:T(8,128)(2,1)S(1)} %update.1), channel_id=1, replica_groups=mesh['x'=4,'zh'=2,'y'=4,'co'=2,'n'=8] {'n'}, dimensions={0} | all-to-all | bytes 262144 | tf_op jit(solution)/shard_map/all_to_all | solution.py:181
  115.7 0.8 order.1
  (1 shorter events, 0.0 us)
Async XLA Ops:
  0.0 0.7 copy-start.5
  0.0 0.7 copy-start.6
  0.7 0.9 copy-start
  1.6 0.8 copy-start.1
  2.4 0.8 copy-start.2
  53.8 9.9 %collective-permute-start = (bf16[4,8,8,8,128]{4,3,2,1,0:T(8,128)(2,1)S(1)}, bf16[4,8,8,8,128]{4,3,2,1,0:T(8,128)(2,1)S(1)}, u32[]{:S(2)}, u32[]{:S(2)}) collective-permute-start(bf16[4,8,8,8,128]{4,3,2,1,0:T(8,128)(2,1)S(1)} %all_to_all.26.own), channel_id=1, source_target_pairs={{0,8},{8,0},{1,9},{9,1},{2,10},{10,2},{3,11},{11,3},{4,12},{12,4},... | collective-permute-start | bytes 1572872 | tf_op jit(solution)/shard_map/ppermute | solution.py:202
  60.3 8.6 %all-to-all-start.3 = ((bf16[8,8,8,128]{3,2,1,0:T(8,128)(2,1)}), bf16[8,8,8,128]{3,2,1,0:T(8,128)(2,1)S(1)}, u32[]{:S(2)}, u32[]{:S(2)}) async-start(bf16[8,8,8,128]{3,2,1,0:T(8,128)(2,1)} %bitcast.6), calls=%async_computation.3 | async-start | bytes 262144 | tf_op jit(solution)/shard_map/all_to_all | solution.py:181
  68.9 20.9 %copy-start.3 = (bf16[128,128]{1,0:T(8,128)(2,1)S(1)}, bf16[128,128]{1,0:T(8,128)(2,1)}, u32[]{:S(2)}) copy-start(bf16[128,128]{1,0:T(8,128)(2,1)} %gate_weight.1) | copy-start | bytes 98308
  68.9 20.9 %copy-start.4 = (bf16[128,128]{1,0:T(8,128)(2,1)S(1)}, bf16[128,128]{1,0:T(8,128)(2,1)}, u32[]{:S(2)}) copy-start(bf16[128,128]{1,0:T(8,128)(2,1)} %out_weight.1) | copy-start | bytes 98308
  68.9 20.9 %all-to-all-start.2 = ((bf16[64,8,128]{2,1,0:T(8,128)(2,1)}), bf16[64,8,128]{2,1,0:T(8,128)(2,1)S(1)}, u32[]{:S(2)}, u32[]{:S(2)}) async-start(bf16[64,8,128]{2,1,0:T(8,128)(2,1)} %bitcast.5), calls=%async_computation.2 | async-start | bytes 262144 | tf_op jit(solution)/shard_map/all_to_all | solution.py:181
  75.0 0.7 collective-permute-start.1
  89.9 0.7 copy-start.7
  89.9 0.7 copy-start.8

commit v2 on v1

v2 whole, which is shorter than its diff:
```python
import jax
import jax.numpy as jnp
from jax import lax
from jax.experimental import pallas as pl
from jax.experimental.pallas import tpu as pltpu
from jax.sharding import Mesh, PartitionSpec as P

F32 = jnp.float32
BF16 = jnp.bfloat16
ROWS = 8
AXES = ("x", "zh", "y", "co", "n")
SPLIT = ("n", "x", "zh")


def params(mib=16):
    return pltpu.CompilerParams(vmem_limit_bytes=mib * 1024 * 1024)


def lane_mask(shape):
    return lax.broadcasted_iota(jnp.int32, shape, len(shape) - 1) < 64


def swap_halves(values):
    return pltpu.roll(values, 64, len(values.shape) - 1)


def cross_halves(first, second):
    low = lane_mask(first.shape)
    return (
        jnp.where(low, first, swap_halves(second)),
        jnp.where(low, swap_halves(first), second),
    )


def layer_norm(values, gain, bias):
    center = jnp.mean(values, axis=-1, keepdims=True)
    moved = values - center
    spread = jnp.mean(moved * moved, axis=-1, keepdims=True)
    return moved * lax.rsqrt(spread + 1e-05) * gain + bias


def edges_kernel(
    pair_hbm, gain_hbm, bias_hbm, left_hbm, right_hbm, last_gain_hbm, last_bias_hbm,
    edges, normed, tall, pair, gain, bias, left_weight, right_weight, last_gain, last_bias, scratch, sems,
):
    moves = [
        pltpu.make_async_copy(source, target, sems.at[slot])
        for slot, (source, target) in enumerate(
            (
                (pair_hbm, pair),
                (gain_hbm, gain),
                (bias_hbm, bias),
                (left_hbm, left_weight),
                (right_hbm, right_weight),
                (last_gain_hbm, last_gain),
                (last_bias_hbm, last_bias),
            )
        )
    ]
    for move in moves:
        move.start()
    for move in moves:
        move.wait()
    values = pair[...].astype(F32).reshape(512, 128)
    rounded = layer_norm(values, gain[...], bias[...]).astype(BF16)
    normed[...] = rounded
    for side, weight in enumerate((left_weight, right_weight)):
        both = lax.dot_general(
            weight[...], rounded, (((0,), (1,)), ((), ())), preferred_element_type=F32
        )
        edge = jax.nn.sigmoid(both[128:]) * both[:128]
        for block in range(4):
            lanes = slice(block * 128, block * 128 + 128)
            even, odd = cross_halves(edge[:64, lanes], edge[64:, lanes])
            start = side * 8 + block * 2
            scratch[pl.ds(start, 64, stride=16), :] = even
            scratch[pl.ds(start + 1, 64, stride=16), :] = odd
    edges[...] = scratch[...].astype(BF16)
    tall[0] = jnp.transpose(jnp.broadcast_to(last_gain[...], (128, 128)))
    tall[1] = jnp.transpose(jnp.broadcast_to(last_bias[...], (128, 128)))


def make_edges(pair, gain, bias, left_weight, right_weight, last_gain, last_bias):
    row = pltpu.VMEM((1, 128), F32)
    return pl.pallas_call(
        edges_kernel,
        out_shape=(
            jax.ShapeDtypeStruct((1024, 128), BF16),
            jax.ShapeDtypeStruct((512, 128), BF16),
            jax.ShapeDtypeStruct((2, 128, 128), F32),
        ),
        in_specs=[pl.BlockSpec(memory_space=pltpu.HBM)] * 7,
        scratch_shapes=[
            pltpu.VMEM((8, 64, 128), BF16),
            row,
            row,
            pltpu.VMEM((128, 256), BF16),
            pltpu.VMEM((128, 256), BF16),
            row,
            row,
            pltpu.VMEM((1024, 128), F32),
            pltpu.SemaphoreType.DMA((7,)),
        ],
        compiler_params=params(63),
        name="edges",
    )(
        pair,
        gain.reshape(1, 128),
        bias.reshape(1, 128),
        left_weight,
        right_weight,
        last_gain.reshape(1, 128),
        last_bias.reshape(1, 128),
    )


def pack_kernel(edges, pair, payload):
    left = edges[:, :8].reshape(512, 128)
    for target in range(4):
        payload[target, :512] = left
        payload[target, 512:] = pair[:, target * 16 : target * 16 + 16].reshape(128, 128)


def make_pack(edges, pair):
    return pl.pallas_call(
        pack_kernel,
        out_shape=jax.ShapeDtypeStruct((4, 640, 128), BF16),
        compiler_params=params(),
        name="pack",
    )(edges, pair)


def triangle_kernel(
    core, own, other, edges, gate_weight, out, gates, normed
):
    first_core = core[0] == 0
    total = jnp.zeros((128, 512), F32)
    for part in range(8):
        rows = slice(part * 64, part * 64 + 64)
        mine = own[:, rows].astype(F32).reshape(4, 8, 8, 128)
        theirs = other[:, rows].astype(F32).reshape(4, 8, 8, 128)
        first = jnp.where(first_core, mine, theirs)
        second = jnp.where(first_core, theirs, mine)
        left = jnp.concatenate(
            [held[y, a] for a in range(8) for y in range(4) for held in (first, second)], axis=0
        ).astype(BF16)
        right = edges[part].astype(F32)[:, 8:].reshape(64, 128)
        low = lane_mask(right.shape)
        right = jnp.concatenate(
            [jnp.where(low, right, 0.0), jnp.where(low, 0.0, right)], axis=0
        ).astype(BF16)
        total += lax.dot_general(
            right, left, (((1,), (1,)), ((), ())), preferred_element_type=F32
        )
    shape = (64, 128)
    low = lane_mask(shape)
    upper = lax.broadcasted_iota(jnp.int32, shape, 0) % 8 < 4
    for block in range(4):
        columns = total[:, block * 128 : block * 128 + 128]
        turned = []
        for hidden in range(2):
            held = columns[hidden * 64 : hidden * 64 + 64]
            up, down = pltpu.roll(held, 60, 0), pltpu.roll(held, 4, 0)
            crossed = swap_halves(jnp.where(upper, up, down))
            turned.append(jnp.where(upper == low, held, crossed))
        even = jnp.where(upper, turned[0], pltpu.roll(turned[1], 4, 0))
        odd = jnp.where(upper, pltpu.roll(turned[0], 60, 0), turned[1])
        out[block * 2] = even.astype(BF16)
        out[block * 2 + 1] = odd.astype(BF16)
    mine = own[:, 512:].astype(F32).reshape(32, 16, 128)
    theirs = other[:, 512:].astype(F32).reshape(32, 16, 128)
    mine = jnp.where(first_core, mine[:, :8], mine[:, 8:]).reshape(4, 64, 128)
    theirs = jnp.where(first_core, theirs[:, :8], theirs[:, 8:]).reshape(4, 64, 128)
    first = jnp.where(first_core, mine, theirs)
    second = jnp.where(first_core, theirs, mine)
    rows = jnp.concatenate([first, second], axis=1).reshape(512, 128)
    normed[...] = rows
    for part in range(4):
        rows = jnp.concatenate(
            [normed[pl.ds(part, 64, stride=8), :], normed[pl.ds(4 + part, 64, stride=8), :]],
            axis=0,
        ).astype(BF16)
        logits = lax.dot_general(
            gate_weight[...], rows, (((0,), (1,)), ((), ())), preferred_element_type=F32
        )
        gates[part] = jax.nn.sigmoid(logits)


def make_triangle(core, own, other, edges, gate_weight):
    return pl.pallas_call(
        triangle_kernel,
        out_shape=(
            jax.ShapeDtypeStruct((8, 64, 128), BF16),
            jax.ShapeDtypeStruct((4, 128, 128), F32),
        ),
        in_specs=[pl.BlockSpec(memory_space=pltpu.SMEM)]
        + [pl.BlockSpec(memory_space=pltpu.VMEM)] * 4,
        scratch_shapes=[pltpu.VMEM((512, 128), F32)],
        compiler_params=params(),
        name="triangle",
    )(core, own, other, edges, gate_weight)


def update_kernel(triangle, gates, out_weight, tall, out, scratch):
    values = triangle[...].astype(F32)
    sums = jnp.sum(values, axis=0)
    squares = jnp.sum(values * values, axis=0)
    center = (sums + pltpu.roll(sums, 4, 0)) / 128
    spread = (squares + pltpu.roll(squares, 4, 0)) / 128 - center * center
    scale = lax.rsqrt(spread + 1e-05)
    scratch[...] = ((values - center) * scale).reshape(512, 128)
    for part in range(4):
        held = jnp.concatenate(
            [
                scratch[pl.ds(part, 64, stride=8), :],
                scratch[pl.ds(4 + part, 64, stride=8), :],
            ],
            axis=0,
        )
        held = (held * tall[0] + tall[1]).astype(BF16)
        projected = lax.dot_general(
            out_weight[...], held, (((0,), (0,)), ((), ())), preferred_element_type=F32
        )
        out[:, part] = (gates[part] * projected).astype(BF16).reshape(8, 16, 128)


def make_update(triangle, gates, out_weight, tall):
    return pl.pallas_call(
        update_kernel,
        out_shape=jax.ShapeDtypeStruct((8, 4, 16, 128), BF16),
        scratch_shapes=[pltpu.VMEM((512, 128), F32)],
        compiler_params=params(),
        name="update",
    )(triangle, gates, out_weight, tall)


def order_kernel(update, out):
    for block in range(4):
        first = update[block * 2].astype(F32).reshape(64, 128)
        second = update[block * 2 + 1].astype(F32).reshape(64, 128)
        upper, lower = cross_halves(first, second)
        lanes = slice(block * 128, block * 128 + 128)
        out[:4, :, lanes] = upper.astype(BF16).reshape(4, 16, 128)
        out[4:, :, lanes] = lower.astype(BF16).reshape(4, 16, 128)


def make_order(update):
    return pl.pallas_call(
        order_kernel,
        out_shape=jax.ShapeDtypeStruct((8, 16, 512), BF16),
        compiler_params=params(),
        name="order",
    )(update)


def exchange(values, axes):
    return lax.all_to_all(values, axes, 0, 0, tiled=True)


def shards(
    pair_rep,
    pair_gain,
    pair_bias,
    left_weight,
    right_weight,
    gate_weight,
    out_weight,
    out_gain,
    out_bias,
):
    swapped = [
        ((a * 8 + e) * 8 + n, (n * 8 + e) * 8 + a)
        for a in range(8)
        for e in range(8)
        for n in range(8)
    ]
    core = lax.axis_index("co").astype(jnp.int32).reshape(1)
    edges, normed, tall = make_edges(
        pair_rep, pair_gain, pair_bias, left_weight, right_weight, out_gain, out_bias
    )
    moved = lax.ppermute(normed.reshape(8, 64, 128), AXES, swapped)
    edges = lax.cond(
        lax.axis_index("x") < 4,
        lambda held: exchange(held, SPLIT),
        lambda held: held,
        edges.reshape(64, 16, 128),
    )
    own = exchange(make_pack(edges, moved), "y")
    other = lax.ppermute(own, "co", [(0, 1), (1, 0)])
    triangle, gates = make_triangle(
        core, own, other, edges.reshape(8, 8, 16, 128), gate_weight
    )
    triangle = exchange(triangle.reshape(64, 8, 128), SPLIT)
    update = make_update(triangle, gates, out_weight, tall)
    return make_order(exchange(update, "n"))


def solution(mesh):
    fine = Mesh(mesh.devices.reshape(4, 2, 4, 2, 8), AXES)
    rows = ("x", "zh", "y", "co")
    in_specs = (P(rows, "n", None), P(), P(), P(), P(), P(), P(), P(), P())
    out_specs = P(rows, "n", None)
    return jax.shard_map(shards, mesh=fine, in_specs=in_specs, out_specs=out_specs, check_vma=False)
```

time: 118 us -> 104 us (0.88)
  waiting for transfers between devices: 18.2 us -> 1.7 us
  blocking collectives: 74.2 us -> 88.7 us
  starting transfers between devices: 16.5 us -> 8.46 us
  local copies, waits for them, and re-layouts: 4.05 us -> 0.03 us
    all_to_all x2 -> x0, waiting for transfers between devices: 18.2 us -> none  [exchange(): return lax.all_to_all(values, axes, 0, 0, tiled=True)]
    all_to_all x3 -> x4, blocking collectives: 74.2 us -> 88.7 us  [exchange(): return lax.all_to_all(values, axes, 0, 0, tiled=True)]
    all_to_all x2 -> x0, starting transfers between devices: 9.35 us -> none  [exchange(): return lax.all_to_all(values, axes, 0, 0, tiled=True)]
    unnamed x18 -> x6, local copies, waits for them, and re-layouts: 3.92 us -> 0.02 us
    ppermute x1, waiting for transfers between devices: 0.01 us -> 1.7 us  [shards(): other = lax.ppermute(own, 'co', [(0, 1), (1, 0)])]
    pallas_call x1, Pallas kernels: 0.91 us -> 2.38 us  [make_edges(): pl.pallas_call(edges_kernel, out_shape=(jax.ShapeDtypeStruct((1024, 128),...]
  transfers between devices with their start and end apart: 4 -> 2, of which waited for: 2 -> 1; matrix products, arithmetic and copies ran while one was open for 0% -> 0% of each run, Pallas kernels for 1% -> 0%
where the time goes in v2:
time: 104 us; the launch traced here: 103 us
  blocking collectives  88.7 us (85%)
  starting transfers between devices  8.46 us (8%)
  Pallas kernels  4.08 us (4%)
  waiting for transfers between devices  1.7 us (2%)
    all_to_all x4, blocking collectives, exchange(): return lax.all_to_all(values, axes, 0, 0, tiled=True)  88.7 us
    ppermute x1, starting transfers between devices, shards(): other = lax.ppermute(own, 'co', [(0, 1), (1, 0)])  6.9 us
    pallas_call x1, Pallas kernels, make_edges(): pl.pallas_call(edges_kernel, out_shape=(jax.ShapeDtypeStruct((1024, 128),...  2.38 us
  transfers between devices with their start and end apart: 2, of which 1 were waited for; matrix products, arithmetic and copies ran while one was open for 0% of the time, Pallas kernels for 0%

profile of v2, /device:TPU:1, one launch (start us, length us, event | category | flops | bytes accessed | tf_op | source)
XLA Modules:
  0.0 103.0 jit_solution(12725324986734344978)
XLA Ops:
  0.0 2.4 %edges.1 = (bf16[1024,128]{1,0:T(8,128)(2,1)S(1)}, bf16[512,128]{1,0:T(8,128)(2,1)}, f32[2,128,128]{2,1,0:T(8,128)}) custom-call(bf16[8,64,128]{2,1,0:T(8,128)(2,1)} %pair_hbm.1, f32[1,128]{1,0:T(1,128)} %bitcast.13, f32[1,128]{1,0:T(1,128)} %bitcast.14, bf16[128,256]{1,0:T(8,128)(2,1)} %left_hbm.1, bf16[128,256]{1,0:T(8,128)(2,1)} %right_hbm.1, ...), custom_call_target="tpu_custom_call" | custom-call | tf_op jit(solution)/shard_map/edges/pallas_call | solution.py:85
  2.4 1.6 %collective-permute-start = (bf16[8,64,128]{2,1,0:T(8,128)(2,1)}, bf16[8,64,128]{2,1,0:T(8,128)(2,1)S(1)}, u32[]{:S(2)}, u32[]{:S(2)}) collective-permute-start(bf16[8,64,128]{2,1,0:T(8,128)(2,1)} %bitcast.17), channel_id=1, source_target_pairs={{0,0},{1,64},{2,128},{3,192},{4,256},{5,320},{6,384},{7,448},{8,8}... | collective-permute-start | bytes 393224 | tf_op jit(solution)/shard_map/ppermute | solution.py:281
  4.0 42.1 %conditional.1 = (bf16[64,16,128]{2,1,0:T(8,128)(2,1)S(1)}) conditional(s32[]{:T(128)} %convert_element_type.3, bf16[64,16,128]{2,1,0:T(8,128)(2,1)S(1)} %bitcast.10, bf16[64,16,128]{2,1,0:T(8,128)(2,1)S(1)} %bitcast.11), branch_computations={%region_0.0_spmd, %region_1.0_spmd} | conditional | bytes 1048584 | solution.py:282
  4.0 42.1 %all_to_all.19 = bf16[64,16,128]{2,1,0:T(8,128)(2,1)S(1)} all-to-all(bf16[64,16,128]{2,1,0:T(8,128)(2,1)S(1)} %copy.12), channel_id=1, replica_groups=mesh['x'=4,'zh'=2,'y'=4,'co'=2,'n'=8] {'n','x','zh'}, dimensions={0} | all-to-all | bytes 524288 | tf_op jit(solution)/shard_map/cond/branch_1_fun/all_to_all | solution.py:257
  46.1 0.0 collective-permute-done.pair
  46.1 0.1 pack.1
  46.2 0.0 copy-start.1
  46.2 11.6 %all_to_all.20.own = bf16[4,640,128]{2,1,0:T(8,128)(2,1)S(1)} all-to-all(bf16[4,640,128]{2,1,0:T(8,128)(2,1)S(1)} %pack.1), channel_id=1, replica_groups=mesh['x'=4,'zh'=2,'y'=4,'co'=2,'n'=8] {'y'}, dimensions={0} | all-to-all | bytes 1310720 | tf_op jit(solution)/shard_map/all_to_all | solution.py:257
  57.8 6.9 %collective-permute-start.1 = (bf16[4,640,128]{2,1,0:T(8,128)(2,1)S(1)}, bf16[4,640,128]{2,1,0:T(8,128)(2,1)S(1)}, u32[]{:S(2)}, u32[]{:S(2)}) collective-permute-start(bf16[4,640,128]{2,1,0:T(8,128)(2,1)S(1)} %all_to_all.20.own), channel_id=1, source_target_pairs={{0,8},{8,0},{1,9},{9,1},{2,10},{10,2},{3,11},{11,3},{4,12},{12,4},... | collective-permute-start | bytes 1966088 | tf_op jit(solution)/shard_map/ppermute | solution.py:289
  64.7 1.7 %collective-permute-done.1.other = bf16[4,640,128]{2,1,0:T(8,128)(2,1)S(1)} collective-permute-done((bf16[4,640,128]{2,1,0:T(8,128)(2,1)S(1)}, bf16[4,640,128]{2,1,0:T(8,128)(2,1)S(1)}, u32[]{:S(2)}, u32[]{:S(2)}) %collective-permute-start.1) | collective-permute-done | bytes 655392 | tf_op jit(solution)/shard_map/ppermute | solution.py:289
  66.4 0.0 copy-done.1
  66.4 0.6 triangle.1
  67.0 0.0 copy-start
  67.0 0.0 copy-start.2
  67.0 20.2 %all_to_all.21.triangle = bf16[64,8,128]{2,1,0:T(8,128)(2,1)S(1)} all-to-all(bf16[64,8,128]{2,1,0:T(8,128)(2,1)S(1)} %bitcast.9), channel_id=1, replica_groups=mesh['x'=4,'zh'=2,'y'=4,'co'=2,'n'=8] {'n','x','zh'}, dimensions={0} | all-to-all | bytes 262144 | tf_op jit(solution)/shard_map/all_to_all | solution.py:257
  87.2 0.0 copy-done
  87.2 0.0 copy-done.2
  87.3 0.3 update.1
  87.6 14.7 %all_to_all.22.update = bf16[8,4,16,128]{3,2,1,0:T(8,128)(2,1)S(1)} all-to-all(bf16[8,4,16,128]{3,2,1,0:T(8,128)(2,1)S(1)} %update.1), channel_id=1, replica_groups=mesh['x'=4,'zh'=2,'y'=4,'co'=2,'n'=8] {'n'}, dimensions={0} | all-to-all | bytes 262144 | tf_op jit(solution)/shard_map/all_to_all | solution.py:257
  102.3 0.8 order.1
  (1 shorter events, 0.0 us)
Async XLA Ops:
  2.4 43.7 %collective-permute-start = (bf16[8,64,128]{2,1,0:T(8,128)(2,1)}, bf16[8,64,128]{2,1,0:T(8,128)(2,1)S(1)}, u32[]{:S(2)}, u32[]{:S(2)}) collective-permute-start(bf16[8,64,128]{2,1,0:T(8,128)(2,1)} %bitcast.17), channel_id=1, source_target_pairs={{0,0},{1,64},{2,128},{3,192},{4,256},{5,320},{6,384},{7,448},{8,8}... | collective-permute-start | bytes 393224 | tf_op jit(solution)/shard_map/ppermute | solution.py:281
  46.2 20.2 %copy-start.1 = (bf16[128,128]{1,0:T(8,128)(2,1)S(1)}, bf16[128,128]{1,0:T(8,128)(2,1)}, u32[]{:S(2)}) copy-start(bf16[128,128]{1,0:T(8,128)(2,1)} %gate_weight.1) | copy-start | bytes 98308
  57.8 8.6 %collective-permute-start.1 = (bf16[4,640,128]{2,1,0:T(8,128)(2,1)S(1)}, bf16[4,640,128]{2,1,0:T(8,128)(2,1)S(1)}, u32[]{:S(2)}, u32[]{:S(2)}) collective-permute-start(bf16[4,640,128]{2,1,0:T(8,128)(2,1)S(1)} %all_to_all.20.own), channel_id=1, source_target_pairs={{0,8},{8,0},{1,9},{9,1},{2,10},{10,2},{3,11},{11,3},{4,12},{12,4},... | collective-permute-start | bytes 1966088 | tf_op jit(solution)/shard_map/ppermute | solution.py:289
  67.0 20.3 %copy-start = (f32[2,128,128]{2,1,0:T(8,128)S(1)}, f32[2,128,128]{2,1,0:T(8,128)}, u32[]{:S(2)}) copy-start(f32[2,128,128]{2,1,0:T(8,128)} %get-tuple-element.25.tall) | copy-start | bytes 393220
  67.0 20.3 %copy-start.2 = (bf16[128,128]{1,0:T(8,128)(2,1)S(1)}, bf16[128,128]{1,0:T(8,128)(2,1)}, u32[]{:S(2)}) copy-start(bf16[128,128]{1,0:T(8,128)(2,1)} %out_weight.1) | copy-start | bytes 98308

commit v3 on v2

--- a/solution.py
+++ b/solution.py
@@ -10,6 +10,18 @@
 ROWS = 8
 AXES = ("x", "zh", "y", "co", "n")
 SPLIT = ("n", "x", "zh")
+
+
+PLACES = (
+    (3, 4, 1, 5, 0, 7, 2, 6),
+    (4, 3, 5, 0, 7, 1, 6, 2),
+    (1, 5, 0, 4, 3, 6, 2, 7),
+    (0, 2, 1, 5, 6, 4, 7, 3),
+    (4, 0, 3, 1, 2, 6, 5, 7),
+    (0, 5, 1, 4, 3, 7, 2, 6),
+    (5, 1, 6, 0, 7, 2, 4, 3),
+    (1, 5, 0, 7, 2, 6, 3, 4),
+)
 
 
 def params(mib=16):
@@ -131,9 +143,9 @@
 
 
 def triangle_kernel(
-    core, own, other, edges, gate_weight, out, gates, normed
+    place, own, other, edges, gate_weight, out, gates, normed
 ):
-    first_core = core[0] == 0
+    first_core = place[0] % 2 == 0
     total = jnp.zeros((128, 512), F32)
     for part in range(8):
         rows = slice(part * 64, part * 64 + 64)
@@ -165,8 +177,10 @@
             turned.append(jnp.where(upper == low, held, crossed))
         even = jnp.where(upper, turned[0], pltpu.roll(turned[1], 4, 0))
         odd = jnp.where(upper, pltpu.roll(turned[0], 60, 0), turned[1])
-        out[block * 2] = even.astype(BF16)
-        out[block * 2 + 1] = odd.astype(BF16)
+        for side, rows in enumerate((even, odd)):
+            rows = rows.astype(BF16).reshape(8, 8, 128)
+            for target in range(8):
+                out[PLACES[target][block * 2 + side], target] = rows[target]
     mine = own[:, 512:].astype(F32).reshape(32, 16, 128)
     theirs = other[:, 512:].astype(F32).reshape(32, 16, 128)
     mine = jnp.where(first_core, mine[:, :8], mine[:, 8:]).reshape(4, 64, 128)
@@ -186,11 +200,11 @@
         gates[part] = jax.nn.sigmoid(logits)
 
 
-def make_triangle(core, own, other, edges, gate_weight):
+def make_triangle(place, own, other, edges, gate_weight):
     return pl.pallas_call(
         triangle_kernel,
         out_shape=(
-            jax.ShapeDtypeStruct((8, 64, 128), BF16),
+            jax.ShapeDtypeStruct((8, 8, 8, 128), BF16),
             jax.ShapeDtypeStruct((4, 128, 128), F32),
         ),
         in_specs=[pl.BlockSpec(memory_space=pltpu.SMEM)]
@@ -198,7 +212,7 @@
         scratch_shapes=[pltpu.VMEM((512, 128), F32)],
         compiler_params=params(),
         name="triangle",
-    )(core, own, other, edges, gate_weight)
+    )(place, own, other, edges, gate_weight)
 
 
 def update_kernel(triangle, gates, out_weight, tall, out, scratch):
@@ -234,23 +248,34 @@
     )(triangle, gates, out_weight, tall)
 
 
-def order_kernel(update, out):
+def order_kernel(place, update, out):
+    own = place[0] // 8
+    held = [PLACES[0][source] for source in range(8)]
+    for target in range(1, 8):
+        held = [
+            jnp.where(own == target, PLACES[target][source], held[source]) for source in range(8)
+        ]
     for block in range(4):
-        first = update[block * 2].astype(F32).reshape(64, 128)
-        second = update[block * 2 + 1].astype(F32).reshape(64, 128)
+        even, odd = held[block * 2], held[block * 2 + 1]
+        first = update[even].astype(F32).reshape(64, 128)
+        second = update[odd].astype(F32).reshape(64, 128)
         upper, lower = cross_halves(first, second)
         lanes = slice(block * 128, block * 128 + 128)
         out[:4, :, lanes] = upper.astype(BF16).reshape(4, 16, 128)
         out[4:, :, lanes] = lower.astype(BF16).reshape(4, 16, 128)
 
 
-def make_order(update):
+def make_order(place, update):
     return pl.pallas_call(
         order_kernel,
         out_shape=jax.ShapeDtypeStruct((8, 16, 512), BF16),
+        in_specs=[
+            pl.BlockSpec(memory_space=pltpu.SMEM),
+            pl.BlockSpec(memory_space=pltpu.VMEM),
+        ],
         compiler_params=params(),
         name="order",
-    )(update)
+    )(place, update)
 
 
 def exchange(values, axes):
@@ -269,12 +294,12 @@
     out_bias,
 ):
     swapped = [
-        ((a * 8 + e) * 8 + n, (n * 8 + e) * 8 + a)
-        for a in range(8)
+        ((s * 8 + e) * 8 + t, (t * 8 + e) * 8 + PLACES[t][s])
+        for s in range(8)
         for e in range(8)
-        for n in range(8)
+        for t in range(8)
     ]
-    core = lax.axis_index("co").astype(jnp.int32).reshape(1)
+    place = lax.axis_index(AXES[:4]).astype(jnp.int32).reshape(1)
     edges, normed, tall = make_edges(
         pair_rep, pair_gain, pair_bias, left_weight, right_weight, out_gain, out_bias
     )
@@ -288,11 +313,11 @@
     own = exchange(make_pack(edges, moved), "y")
     other = lax.ppermute(own, "co", [(0, 1), (1, 0)])
     triangle, gates = make_triangle(
-        core, own, other, edges.reshape(8, 8, 16, 128), gate_weight
+        place, own, other, edges.reshape(8, 8, 16, 128), gate_weight
     )
     triangle = exchange(triangle.reshape(64, 8, 128), SPLIT)
     update = make_update(triangle, gates, out_weight, tall)
-    return make_order(exchange(update, "n"))
+    return make_order(place, exchange(update, "n"))
 
 
 def solution(mesh):

time: 104 us -> 103 us (level)
  blocking collectives: 88.7 us -> 82.2 us
  starting transfers between devices: 8.46 us -> 14.1 us
    all_to_all x4, blocking collectives: 88.7 us -> 82.2 us  [exchange(): return lax.all_to_all(values, axes, 0, 0, tiled=True)]
    ppermute x1, starting transfers between devices: 1.56 us -> 7.08 us  [shards(): moved = lax.ppermute(normed.reshape(8, 64, 128), AXES, swapped)]
where the time goes in v3:
time: 103 us; the launch traced here: 102 us
  blocking collectives  82.2 us (80%)
  starting transfers between devices  14.1 us (14%)
  Pallas kernels  4.08 us (4%)
  waiting for transfers between devices  1.69 us (2%)
    all_to_all x4, blocking collectives, exchange(): return lax.all_to_all(values, axes, 0, 0, tiled=True)  82.2 us
    ppermute x1, starting transfers between devices, shards(): moved = lax.ppermute(normed.reshape(8, 64, 128), AXES, swapped)  7.08 us
    ppermute x1, starting transfers between devices, shards(): other = lax.ppermute(own, 'co', [(0, 1), (1, 0)])  7.04 us
    pallas_call x1, Pallas kernels, make_edges(): pl.pallas_call(edges_kernel, out_shape=(jax.ShapeDtypeStruct((1024, 128),...  2.38 us
  transfers between devices with their start and end apart: 2, of which 1 were waited for; matrix products, arithmetic and copies ran while one was open for 0% of the time, Pallas kernels for 0%

profile of v3, /device:TPU:1, one launch (start us, length us, event | category | flops | bytes accessed | tf_op | source)
XLA Modules:
  0.0 102.2 jit_solution(12743062245720201911)
XLA Ops:
  0.0 2.4 %edges.1 = (bf16[1024,128]{1,0:T(8,128)(2,1)S(1)}, bf16[512,128]{1,0:T(8,128)(2,1)}, f32[2,128,128]{2,1,0:T(8,128)}) custom-call(bf16[8,64,128]{2,1,0:T(8,128)(2,1)} %pair_hbm.1, f32[1,128]{1,0:T(1,128)} %bitcast.13, f32[1,128]{1,0:T(1,128)} %bitcast.14, bf16[128,256]{1,0:T(8,128)(2,1)} %left_hbm.1, bf16[128,256]{1,0:T(8,128)(2,1)} %right_hbm.1, ...), custom_call_target="tpu_custom_call" | custom-call | tf_op jit(solution)/shard_map/edges/pallas_call | solution.py:97
  2.4 7.1 %collective-permute-start = (bf16[8,64,128]{2,1,0:T(8,128)(2,1)}, bf16[8,64,128]{2,1,0:T(8,128)(2,1)S(1)}, u32[]{:S(2)}, u32[]{:S(2)}) collective-permute-start(bf16[8,64,128]{2,1,0:T(8,128)(2,1)} %bitcast.17), channel_id=1, source_target_pairs={{0,3},{1,68},{2,129},{3,192},{4,260},{5,320},{6,389},{7,449},{8,11... | collective-permute-start | bytes 393224 | tf_op jit(solution)/shard_map/ppermute | solution.py:306
  9.5 35.7 %conditional.1 = (bf16[64,16,128]{2,1,0:T(8,128)(2,1)S(1)}) conditional(s32[]{:T(128)} %convert_element_type.3, bf16[64,16,128]{2,1,0:T(8,128)(2,1)S(1)} %bitcast.10, bf16[64,16,128]{2,1,0:T(8,128)(2,1)S(1)} %bitcast.11), branch_computations={%region_0.0_spmd, %region_1.0_spmd} | conditional | bytes 1048584 | solution.py:307
  9.5 35.7 %all_to_all.19 = bf16[64,16,128]{2,1,0:T(8,128)(2,1)S(1)} all-to-all(bf16[64,16,128]{2,1,0:T(8,128)(2,1)S(1)} %copy.12), channel_id=1, replica_groups=mesh['x'=4,'zh'=2,'y'=4,'co'=2,'n'=8] {'n','x','zh'}, dimensions={0} | all-to-all | bytes 524288 | tf_op jit(solution)/shard_map/cond/branch_1_fun/all_to_all | solution.py:282
  45.2 0.0 collective-permute-done.pair
  45.2 0.1 pack.1
  45.3 11.6 %all_to_all.20.own = bf16[4,640,128]{2,1,0:T(8,128)(2,1)S(1)} all-to-all(bf16[4,640,128]{2,1,0:T(8,128)(2,1)S(1)} %pack.1), channel_id=1, replica_groups=mesh['x'=4,'zh'=2,'y'=4,'co'=2,'n'=8] {'y'}, dimensions={0} | all-to-all | bytes 1310720 | tf_op jit(solution)/shard_map/all_to_all | solution.py:282
  56.9 0.0 copy-start.1
  56.9 7.0 %collective-permute-start.1 = (bf16[4,640,128]{2,1,0:T(8,128)(2,1)S(1)}, bf16[4,640,128]{2,1,0:T(8,128)(2,1)S(1)}, u32[]{:S(2)}, u32[]{:S(2)}) collective-permute-start(bf16[4,640,128]{2,1,0:T(8,128)(2,1)S(1)} %all_to_all.20.own), channel_id=1, source_target_pairs={{0,8},{8,0},{1,9},{9,1},{2,10},{10,2},{3,11},{11,3},{4,12},{12,4},... | collective-permute-start | bytes 1966088 | tf_op jit(solution)/shard_map/ppermute | solution.py:314
  63.9 1.7 %collective-permute-done.1.other = bf16[4,640,128]{2,1,0:T(8,128)(2,1)S(1)} collective-permute-done((bf16[4,640,128]{2,1,0:T(8,128)(2,1)S(1)}, bf16[4,640,128]{2,1,0:T(8,128)(2,1)S(1)}, u32[]{:S(2)}, u32[]{:S(2)}) %collective-permute-start.1) | collective-permute-done | bytes 655392 | tf_op jit(solution)/shard_map/ppermute | solution.py:314
  65.6 0.0 copy-done.1
  65.6 0.6 triangle.1
  66.2 0.0 copy-start
  66.2 0.0 copy-start.2
  66.2 20.3 %all_to_all.21.triangle = bf16[64,8,128]{2,1,0:T(8,128)(2,1)S(1)} all-to-all(bf16[64,8,128]{2,1,0:T(8,128)(2,1)S(1)} %bitcast.9), channel_id=1, replica_groups=mesh['x'=4,'zh'=2,'y'=4,'co'=2,'n'=8] {'n','x','zh'}, dimensions={0} | all-to-all | bytes 262144 | tf_op jit(solution)/shard_map/all_to_all | solution.py:282
  86.5 0.0 copy-done
  86.5 0.0 copy-done.2
  86.5 0.3 update.1
  86.8 14.7 %all_to_all.22.update = bf16[8,4,16,128]{3,2,1,0:T(8,128)(2,1)S(1)} all-to-all(bf16[8,4,16,128]{3,2,1,0:T(8,128)(2,1)S(1)} %update.1), channel_id=1, replica_groups=mesh['x'=4,'zh'=2,'y'=4,'co'=2,'n'=8] {'n'}, dimensions={0} | all-to-all | bytes 262144 | tf_op jit(solution)/shard_map/all_to_all | solution.py:282
  101.5 0.8 order.1
  (1 shorter events, 0.0 us)
Async XLA Ops:
  2.4 42.8 %collective-permute-start = (bf16[8,64,128]{2,1,0:T(8,128)(2,1)}, bf16[8,64,128]{2,1,0:T(8,128)(2,1)S(1)}, u32[]{:S(2)}, u32[]{:S(2)}) collective-permute-start(bf16[8,64,128]{2,1,0:T(8,128)(2,1)} %bitcast.17), channel_id=1, source_target_pairs={{0,3},{1,68},{2,129},{3,192},{4,260},{5,320},{6,389},{7,449},{8,11... | collective-permute-start | bytes 393224 | tf_op jit(solution)/shard_map/ppermute | solution.py:306
  56.9 8.8 %copy-start.1 = (bf16[128,128]{1,0:T(8,128)(2,1)S(1)}, bf16[128,128]{1,0:T(8,128)(2,1)}, u32[]{:S(2)}) copy-start(bf16[128,128]{1,0:T(8,128)(2,1)} %gate_weight.1) | copy-start | bytes 98308
  56.9 8.7 %collective-permute-start.1 = (bf16[4,640,128]{2,1,0:T(8,128)(2,1)S(1)}, bf16[4,640,128]{2,1,0:T(8,128)(2,1)S(1)}, u32[]{:S(2)}, u32[]{:S(2)}) collective-permute-start(bf16[4,640,128]{2,1,0:T(8,128)(2,1)S(1)} %all_to_all.20.own), channel_id=1, source_target_pairs={{0,8},{8,0},{1,9},{9,1},{2,10},{10,2},{3,11},{11,3},{4,12},{12,4},... | collective-permute-start | bytes 1966088 | tf_op jit(solution)/shard_map/ppermute | solution.py:314
  66.2 20.3 %copy-start = (f32[2,128,128]{2,1,0:T(8,128)S(1)}, f32[2,128,128]{2,1,0:T(8,128)}, u32[]{:S(2)}) copy-start(f32[2,128,128]{2,1,0:T(8,128)} %get-tuple-element.25.tall) | copy-start | bytes 393220
  66.2 20.3 %copy-start.2 = (bf16[128,128]{1,0:T(8,128)(2,1)S(1)}, bf16[128,128]{1,0:T(8,128)(2,1)}, u32[]{:S(2)}) copy-start(bf16[128,128]{1,0:T(8,128)(2,1)} %out_weight.1) | copy-start | bytes 98308

commit v4 on v3

--- a/solution.py
+++ b/solution.py
@@ -53,7 +53,7 @@
 
 def edges_kernel(
     pair_hbm, gain_hbm, bias_hbm, left_hbm, right_hbm, last_gain_hbm, last_bias_hbm,
-    edges, normed, tall, pair, gain, bias, left_weight, right_weight, last_gain, last_bias, scratch, sems,
+    edges, normed_hbm, tall_hbm, pair, gain, bias, left_weight, right_weight, last_gain, last_bias, scratch, normed, tall, sems,
 ):
     moves = [
         pltpu.make_async_copy(source, target, sems.at[slot])
@@ -76,6 +76,14 @@
     values = pair[...].astype(F32).reshape(512, 128)
     rounded = layer_norm(values, gain[...], bias[...]).astype(BF16)
     normed[...] = rounded
+    tall[0] = jnp.transpose(jnp.broadcast_to(last_gain[...], (128, 128)))
+    tall[1] = jnp.transpose(jnp.broadcast_to(last_bias[...], (128, 128)))
+    results = [
+        pltpu.make_async_copy(normed, normed_hbm, sems.at[7]),
+        pltpu.make_async_copy(tall, tall_hbm, sems.at[8]),
+    ]
+    for result in results:
+        result.start()
     for side, weight in enumerate((left_weight, right_weight)):
         both = lax.dot_general(
             weight[...], rounded, (((0,), (1,)), ((), ())), preferred_element_type=F32
@@ -88,8 +96,8 @@
             scratch[pl.ds(start, 64, stride=16), :] = even
             scratch[pl.ds(start + 1, 64, stride=16), :] = odd
     edges[...] = scratch[...].astype(BF16)
-    tall[0] = jnp.transpose(jnp.broadcast_to(last_gain[...], (128, 128)))
-    tall[1] = jnp.transpose(jnp.broadcast_to(last_bias[...], (128, 128)))
+    for result in results:
+        result.wait()
 
 
 def make_edges(pair, gain, bias, left_weight, right_weight, last_gain, last_bias):
@@ -102,6 +110,11 @@
             jax.ShapeDtypeStruct((2, 128, 128), F32),
         ),
         in_specs=[pl.BlockSpec(memory_space=pltpu.HBM)] * 7,
+        out_specs=(
+            pl.BlockSpec(memory_space=pltpu.VMEM),
+            pl.BlockSpec(memory_space=pltpu.HBM),
+            pl.BlockSpec(memory_space=pltpu.HBM),
+        ),
         scratch_shapes=[
             pltpu.VMEM((8, 64, 128), BF16),
             row,
@@ -111,7 +124,9 @@
             row,
             row,
             pltpu.VMEM((1024, 128), F32),
-            pltpu.SemaphoreType.DMA((7,)),
+            pltpu.VMEM((512, 128), BF16),
+            pltpu.VMEM((2, 128, 128), F32),
+            pltpu.SemaphoreType.DMA((9,)),
         ],
         compiler_params=params(63),
         name="edges",

time: 103 us -> 103 us (level)
  no operation moved by 1% of the time
where the time goes in v4:
time: 103 us; the launch traced here: 102 us
  blocking collectives  82.2 us (80%)
  starting transfers between devices  14.1 us (14%)
  Pallas kernels  3.81 us (4%)
  waiting for transfers between devices  1.69 us (2%)
    all_to_all x4, blocking collectives, exchange(): return lax.all_to_all(values, axes, 0, 0, tiled=True)  82.2 us
    ppermute x1, starting transfers between devices, shards(): moved = lax.ppermute(normed.reshape(8, 64, 128), AXES, swapped)  7.08 us
    ppermute x1, starting transfers between devices, shards(): other = lax.ppermute(own, 'co', [(0, 1), (1, 0)])  7.03 us
    pallas_call x1, Pallas kernels, make_edges(): pl.pallas_call(edges_kernel, out_shape=(jax.ShapeDtypeStruct((1024, 128),...  2.11 us
  transfers between devices with their start and end apart: 2, of which 1 were waited for; matrix products, arithmetic and copies ran while one was open for 0% of the time, Pallas kernels for 0%

profile of v4, /device:TPU:1, one launch (start us, length us, event | category | flops | bytes accessed | tf_op | source)
XLA Modules:
  0.0 102.0 jit_solution(11431754979743574428)
XLA Ops:
  0.0 2.1 %edges.1 = (bf16[1024,128]{1,0:T(8,128)(2,1)S(1)}, bf16[512,128]{1,0:T(8,128)(2,1)}, f32[2,128,128]{2,1,0:T(8,128)}) custom-call(bf16[8,64,128]{2,1,0:T(8,128)(2,1)} %pair_hbm.1, f32[1,128]{1,0:T(1,128)} %bitcast.13, f32[1,128]{1,0:T(1,128)} %bitcast.14, bf16[128,256]{1,0:T(8,128)(2,1)} %left_hbm.1, bf16[128,256]{1,0:T(8,128)(2,1)} %right_hbm.1, ...), custom_call_target="tpu_custom_call" | custom-call | tf_op jit(solution)/shard_map/edges/pallas_call | solution.py:105
  2.1 7.1 %collective-permute-start = (bf16[8,64,128]{2,1,0:T(8,128)(2,1)}, bf16[8,64,128]{2,1,0:T(8,128)(2,1)S(1)}, u32[]{:S(2)}, u32[]{:S(2)}) collective-permute-start(bf16[8,64,128]{2,1,0:T(8,128)(2,1)} %bitcast.17), channel_id=1, source_target_pairs={{0,3},{1,68},{2,129},{3,192},{4,260},{5,320},{6,389},{7,449},{8,11... | collective-permute-start | bytes 393224 | tf_op jit(solution)/shard_map/ppermute | solution.py:321
  9.2 35.7 %conditional.1 = (bf16[64,16,128]{2,1,0:T(8,128)(2,1)S(1)}) conditional(s32[]{:T(128)} %convert_element_type.3, bf16[64,16,128]{2,1,0:T(8,128)(2,1)S(1)} %bitcast.10, bf16[64,16,128]{2,1,0:T(8,128)(2,1)S(1)} %bitcast.11), branch_computations={%region_0.0_spmd, %region_1.0_spmd} | conditional | bytes 1048584 | solution.py:322
  9.3 35.6 %all_to_all.19 = bf16[64,16,128]{2,1,0:T(8,128)(2,1)S(1)} all-to-all(bf16[64,16,128]{2,1,0:T(8,128)(2,1)S(1)} %copy.12), channel_id=1, replica_groups=mesh['x'=4,'zh'=2,'y'=4,'co'=2,'n'=8] {'n','x','zh'}, dimensions={0} | all-to-all | bytes 524288 | tf_op jit(solution)/shard_map/cond/branch_1_fun/all_to_all | solution.py:297
  44.9 0.0 collective-permute-done.pair
  44.9 0.1 pack.1
  45.0 11.6 %all_to_all.20.own = bf16[4,640,128]{2,1,0:T(8,128)(2,1)S(1)} all-to-all(bf16[4,640,128]{2,1,0:T(8,128)(2,1)S(1)} %pack.1), channel_id=1, replica_groups=mesh['x'=4,'zh'=2,'y'=4,'co'=2,'n'=8] {'y'}, dimensions={0} | all-to-all | bytes 1310720 | tf_op jit(solution)/shard_map/all_to_all | solution.py:297
  56.6 0.0 copy-start.1
  56.6 7.0 %collective-permute-start.1 = (bf16[4,640,128]{2,1,0:T(8,128)(2,1)S(1)}, bf16[4,640,128]{2,1,0:T(8,128)(2,1)S(1)}, u32[]{:S(2)}, u32[]{:S(2)}) collective-permute-start(bf16[4,640,128]{2,1,0:T(8,128)(2,1)S(1)} %all_to_all.20.own), channel_id=1, source_target_pairs={{0,8},{8,0},{1,9},{9,1},{2,10},{10,2},{3,11},{11,3},{4,12},{12,4},... | collective-permute-start | bytes 1966088 | tf_op jit(solution)/shard_map/ppermute | solution.py:329
  63.7 1.7 %collective-permute-done.1.other = bf16[4,640,128]{2,1,0:T(8,128)(2,1)S(1)} collective-permute-done((bf16[4,640,128]{2,1,0:T(8,128)(2,1)S(1)}, bf16[4,640,128]{2,1,0:T(8,128)(2,1)S(1)}, u32[]{:S(2)}, u32[]{:S(2)}) %collective-permute-start.1) | collective-permute-done | bytes 655392 | tf_op jit(solution)/shard_map/ppermute | solution.py:329
  65.4 0.0 copy-done.1
  65.4 0.6 triangle.1
  65.9 0.0 copy-start
  65.9 0.0 copy-start.2
  65.9 20.2 %all_to_all.21.triangle = bf16[64,8,128]{2,1,0:T(8,128)(2,1)S(1)} all-to-all(bf16[64,8,128]{2,1,0:T(8,128)(2,1)S(1)} %bitcast.9), channel_id=1, replica_groups=mesh['x'=4,'zh'=2,'y'=4,'co'=2,'n'=8] {'n','x','zh'}, dimensions={0} | all-to-all | bytes 262144 | tf_op jit(solution)/shard_map/all_to_all | solution.py:297
  86.2 0.0 copy-done
  86.2 0.0 copy-done.2
  86.2 0.3 update.1
  86.5 14.7 %all_to_all.22.update = bf16[8,4,16,128]{3,2,1,0:T(8,128)(2,1)S(1)} all-to-all(bf16[8,4,16,128]{3,2,1,0:T(8,128)(2,1)S(1)} %update.1), channel_id=1, replica_groups=mesh['x'=4,'zh'=2,'y'=4,'co'=2,'n'=8] {'n'}, dimensions={0} | all-to-all | bytes 262144 | tf_op jit(solution)/shard_map/all_to_all | solution.py:297
  101.2 0.8 order.1
  (1 shorter events, 0.0 us)
Async XLA Ops:
  2.1 42.8 %collective-permute-start = (bf16[8,64,128]{2,1,0:T(8,128)(2,1)}, bf16[8,64,128]{2,1,0:T(8,128)(2,1)S(1)}, u32[]{:S(2)}, u32[]{:S(2)}) collective-permute-start(bf16[8,64,128]{2,1,0:T(8,128)(2,1)} %bitcast.17), channel_id=1, source_target_pairs={{0,3},{1,68},{2,129},{3,192},{4,260},{5,320},{6,389},{7,449},{8,11... | collective-permute-start | bytes 393224 | tf_op jit(solution)/shard_map/ppermute | solution.py:321
  56.6 8.7 %copy-start.1 = (bf16[128,128]{1,0:T(8,128)(2,1)S(1)}, bf16[128,128]{1,0:T(8,128)(2,1)}, u32[]{:S(2)}) copy-start(bf16[128,128]{1,0:T(8,128)(2,1)} %gate_weight.1) | copy-start | bytes 98308
  56.6 8.7 %collective-permute-start.1 = (bf16[4,640,128]{2,1,0:T(8,128)(2,1)S(1)}, bf16[4,640,128]{2,1,0:T(8,128)(2,1)S(1)}, u32[]{:S(2)}, u32[]{:S(2)}) collective-permute-start(bf16[4,640,128]{2,1,0:T(8,128)(2,1)S(1)} %all_to_all.20.own), channel_id=1, source_target_pairs={{0,8},{8,0},{1,9},{9,1},{2,10},{10,2},{3,11},{11,3},{4,12},{12,4},... | collective-permute-start | bytes 1966088 | tf_op jit(solution)/shard_map/ppermute | solution.py:329
  65.9 20.3 %copy-start = (f32[2,128,128]{2,1,0:T(8,128)S(1)}, f32[2,128,128]{2,1,0:T(8,128)}, u32[]{:S(2)}) copy-start(f32[2,128,128]{2,1,0:T(8,128)} %get-tuple-element.25.tall) | copy-start | bytes 393220
  65.9 20.3 %copy-start.2 = (bf16[128,128]{1,0:T(8,128)(2,1)S(1)}, bf16[128,128]{1,0:T(8,128)(2,1)}, u32[]{:S(2)}) copy-start(bf16[128,128]{1,0:T(8,128)(2,1)} %out_weight.1) | copy-start | bytes 98308

commit v5 on v4

--- a/solution.py
+++ b/solution.py
@@ -1,5 +1,6 @@
 import jax
 import jax.numpy as jnp
+import numpy as np
 from jax import lax
 from jax.experimental import pallas as pl
 from jax.experimental.pallas import tpu as pltpu
@@ -141,81 +142,72 @@
     )
 
 
-def pack_kernel(edges, pair, payload):
+def pack_kernel(edges, pair, payload, right):
     left = edges[:, :8].reshape(512, 128)
     for target in range(4):
         payload[target, :512] = left
         payload[target, 512:] = pair[:, target * 16 : target * 16 + 16].reshape(128, 128)
+    right[...] = edges[:, 8:].reshape(512, 128)
 
 
 def make_pack(edges, pair):
     return pl.pallas_call(
         pack_kernel,
-        out_shape=jax.ShapeDtypeStruct((4, 640, 128), BF16),
+        out_shape=(
+            jax.ShapeDtypeStruct((4, 640, 128), BF16),
+            jax.ShapeDtypeStruct((512, 128), BF16),
+        ),
         compiler_params=params(),
         name="pack",
     )(edges, pair)
 
 
-def triangle_kernel(
-    place, own, other, edges, gate_weight, out, gates, normed
-):
+def triangle_kernel(place, received, right, other, gate_weight, out, gates, normed, rows):
     first_core = place[0] % 2 == 0
-    total = jnp.zeros((128, 512), F32)
+    total = jnp.zeros((256, 256), F32)
     for part in range(8):
-        rows = slice(part * 64, part * 64 + 64)
-        mine = own[:, rows].astype(F32).reshape(4, 8, 8, 128)
-        theirs = other[:, rows].astype(F32).reshape(4, 8, 8, 128)
-        first = jnp.where(first_core, mine, theirs)
-        second = jnp.where(first_core, theirs, mine)
-        left = jnp.concatenate(
-            [held[y, a] for a in range(8) for y in range(4) for held in (first, second)], axis=0
+        mine = right[part * 64 : part * 64 + 64].astype(F32)
+        theirs = other[part * 64 : part * 64 + 64].astype(F32)
+        low = lane_mask(mine.shape)
+        sides = (jnp.where(first_core, mine, theirs), jnp.where(first_core, theirs, mine))
+        halves = [jnp.where(low, side, 0.0) for side in sides]
+        halves += [jnp.where(low, 0.0, side) for side in sides]
+        right_rows = jnp.concatenate(
+            [half[a * 8 : a * 8 + 8] for a in range(8) for half in halves], axis=0
         ).astype(BF16)
-        right = edges[part].astype(F32)[:, 8:].reshape(64, 128)
-        low = lane_mask(right.shape)
-        right = jnp.concatenate(
-            [jnp.where(low, right, 0.0), jnp.where(low, 0.0, right)], axis=0
+        held = received[:, part * 64 : part * 64 + 64].astype(F32)
+        left_rows = jnp.concatenate(
+            [held[y, a * 8 : a * 8 + 8] for a in range(8) for y in range(4)], axis=0
         ).astype(BF16)
         total += lax.dot_general(
-            right, left, (((1,), (1,)), ((), ())), preferred_element_type=F32
-        )
-    shape = (64, 128)
-    low = lane_mask(shape)
-    upper = lax.broadcasted_iota(jnp.int32, shape, 0) % 8 < 4
-    for block in range(4):
-        columns = total[:, block * 128 : block * 128 + 128]
-        turned = []
-        for hidden in range(2):
-            held = columns[hidden * 64 : hidden * 64 + 64]
-            up, down = pltpu.roll(held, 60, 0), pltpu.roll(held, 4, 0)
-            crossed = swap_halves(jnp.where(upper, up, down))
-            turned.append(jnp.where(upper == low, held, crossed))
-        even = jnp.where(upper, turned[0], pltpu.roll(turned[1], 4, 0))
-        odd = jnp.where(upper, pltpu.roll(turned[0], 60, 0), turned[1])
-        for side, rows in enumerate((even, odd)):
-            rows = rows.astype(BF16).reshape(8, 8, 128)
+            right_rows, left_rows, (((1,), (1,)), ((), ())), preferred_element_type=F32
+        )
+    lane_group = lax.broadcasted_iota(jnp.int32, (64, 128), 1) // 32
+    for block in range(2):
+        rows[block] = total[:, block * 128 : block * 128 + 128]
+        taken = [rows[block, pl.ds(row, 64, stride=4), :] for row in range(4)]
+        for group in range(4):
+            turned = taken[0] if group == 0 else pltpu.roll(taken[0], 128 - group * 32, 1)
+            for row in range(1, 4):
+                shift = (row - group) * 32 % 128
+                rolled = pltpu.roll(taken[row], shift, 1) if shift else taken[row]
+                turned = jnp.where(lane_group == row, rolled, turned)
+            turned = turned.astype(BF16).reshape(8, 8, 128)
             for target in range(8):
-                out[PLACES[target][block * 2 + side], target] = rows[target]
-    mine = own[:, 512:].astype(F32).reshape(32, 16, 128)
-    theirs = other[:, 512:].astype(F32).reshape(32, 16, 128)
-    mine = jnp.where(first_core, mine[:, :8], mine[:, 8:]).reshape(4, 64, 128)
-    theirs = jnp.where(first_core, theirs[:, :8], theirs[:, 8:]).reshape(4, 64, 128)
-    first = jnp.where(first_core, mine, theirs)
-    second = jnp.where(first_core, theirs, mine)
-    rows = jnp.concatenate([first, second], axis=1).reshape(512, 128)
-    normed[...] = rows
+                out[PLACES[target][block * 4 + group], target] = turned[target]
+    normed[...] = received[:, 512:].astype(F32).reshape(512, 128)
     for part in range(4):
-        rows = jnp.concatenate(
-            [normed[pl.ds(part, 64, stride=8), :], normed[pl.ds(4 + part, 64, stride=8), :]],
-            axis=0,
+        first = part // 2 * 8 + part % 2 * 4
+        pairs = jnp.concatenate(
+            [normed[pl.ds(first + row, 32, stride=16), :] for row in range(4)], axis=0
         ).astype(BF16)
         logits = lax.dot_general(
-            gate_weight[...], rows, (((0,), (1,)), ((), ())), preferred_element_type=F32
+            gate_weight[...], pairs, (((0,), (1,)), ((), ())), preferred_element_type=F32
         )
         gates[part] = jax.nn.sigmoid(logits)
 
 
-def make_triangle(place, own, other, edges, gate_weight):
+def make_triangle(place, received, right, other, gate_weight):
     return pl.pallas_call(
         triangle_kernel,
         out_shape=(
@@ -224,10 +216,10 @@
         ),
         in_specs=[pl.BlockSpec(memory_space=pltpu.SMEM)]
         + [pl.BlockSpec(memory_space=pltpu.VMEM)] * 4,
-        scratch_shapes=[pltpu.VMEM((512, 128), F32)],
+        scratch_shapes=[pltpu.VMEM((512, 128), F32), pltpu.VMEM((2, 256, 128), F32)],
         compiler_params=params(),
         name="triangle",
-    )(place, own, other, edges, gate_weight)
+    )(place, received, right, other, gate_weight)
 
 
 def update_kernel(triangle, gates, out_weight, tall, out, scratch):
@@ -250,34 +242,50 @@
         projected = lax.dot_general(
             out_weight[...], held, (((0,), (0,)), ((), ())), preferred_element_type=F32
         )
-        out[:, part] = (gates[part] * projected).astype(BF16).reshape(8, 16, 128)
+        update = (gates[part] * projected).astype(BF16)
+        out[part // 2, :, part % 2] = update.reshape(8, 16, 128)
 
 
 def make_update(triangle, gates, out_weight, tall):
     return pl.pallas_call(
         update_kernel,
-        out_shape=jax.ShapeDtypeStruct((8, 4, 16, 128), BF16),
+        out_shape=jax.ShapeDtypeStruct((2, 8, 2, 16, 128), BF16),
         scratch_shapes=[pltpu.VMEM((512, 128), F32)],
         compiler_params=params(),
         name="update",
     )(triangle, gates, out_weight, tall)
 
 
-def order_kernel(place, update, out):
+def order_matrix():
+    lanes = np.arange(512).reshape(2, 2, 4, 4, 8).transpose(2, 0, 3, 1, 4).reshape(512)
+    return (np.arange(512)[:, None] == lanes[None, :]).astype(jnp.bfloat16)
+
+
+def order_kernel(place, update, matrix, out):
     own = place[0] // 8
     held = [PLACES[0][source] for source in range(8)]
     for target in range(1, 8):
         held = [
             jnp.where(own == target, PLACES[target][source], held[source]) for source in range(8)
         ]
+    pieces = [
+        jnp.concatenate(
+            [update[core * 8 + held[block * 2 + side], half] for side in range(2) for core in range(2)],
+            axis=1,
+        )
+        for block in range(4)
+        for half in range(2)
+    ]
+    turned = jnp.dot(
+        jnp.concatenate(pieces, axis=0), matrix[...], preferred_element_type=F32
+    ).astype(BF16)
     for block in range(4):
-        even, odd = held[block * 2], held[block * 2 + 1]
-        first = update[even].astype(F32).reshape(64, 128)
-        second = update[odd].astype(F32).reshape(64, 128)
-        upper, lower = cross_halves(first, second)
-        lanes = slice(block * 128, block * 128 + 128)
-        out[:4, :, lanes] = upper.astype(BF16).reshape(4, 16, 128)
-        out[4:, :, lanes] = lower.astype(BF16).reshape(4, 16, 128)
+        for half in range(2):
+            rows = (block * 2 + half) * 16
+            for row in range(4):
+                out[half * 4 + row, :, block * 128 : block * 128 + 128] = turned[
+                    rows : rows + 16, row * 128 : row * 128 + 128
+                ]
 
 
 def make_order(place, update):
@@ -287,10 +295,11 @@
         in_specs=[
             pl.BlockSpec(memory_space=pltpu.SMEM),
             pl.BlockSpec(memory_space=pltpu.VMEM),
+            pl.BlockSpec(memory_space=pltpu.VMEM),
         ],
         compiler_params=params(),
         name="order",
-    )(place, update)
+    )(place, update, jnp.asarray(order_matrix()))
 
 
 def exchange(values, axes):
@@ -325,14 +334,13 @@
         lambda held: held,
         edges.reshape(64, 16, 128),
     )
-    own = exchange(make_pack(edges, moved), "y")
-    other = lax.ppermute(own, "co", [(0, 1), (1, 0)])
-    triangle, gates = make_triangle(
-        place, own, other, edges.reshape(8, 8, 16, 128), gate_weight
-    )
+    payload, right = make_pack(edges, moved)
+    received = exchange(payload, "y")
+    other = lax.ppermute(right, "co", [(0, 1), (1, 0)])
+    triangle, gates = make_triangle(place, received, right, other, gate_weight)
     triangle = exchange(triangle.reshape(64, 8, 128), SPLIT)
     update = make_update(triangle, gates, out_weight, tall)
-    return make_order(place, exchange(update, "n"))
+    return make_order(place, exchange(update.reshape(16, 2, 16, 128), ("co", "n")))
 
 
 def solution(mesh):

time: 103 us -> 101 us (0.981); the launches traced: 102 us -> 101 us
  blocking collectives: 82.2 us -> 77.1 us
  starting transfers between devices: 14.1 us -> 17.1 us
  Pallas kernels: 3.81 us -> 4.91 us
    all_to_all x4 -> x3, blocking collectives: 82.2 us -> 77.1 us  [exchange(): return lax.all_to_all(values, axes, 0, 0, tiled=True)]
    all_to_all x0 -> x1, starting transfers between devices: none -> 4.19 us  [exchange(): return lax.all_to_all(values, axes, 0, 0, tiled=True)]
    ppermute x1, starting transfers between devices: 7.03 us -> 5.88 us  [shards(): other = lax.ppermute(right, 'co', [(0, 1), (1, 0)])]
  transfers between devices with their start and end apart: 2 -> 3, of which waited for: 1 -> 2; matrix products, arithmetic and copies ran while one was open for 0% -> 0% of each run, Pallas kernels for 0% -> 0%
where the time goes in v5:
time: 101 us
  blocking collectives  77.1 us (76%)
  starting transfers between devices  17.1 us (17%)
  Pallas kernels  4.91 us (5%)
  waiting for transfers between devices  1.74 us (2%)
    all_to_all x3, blocking collectives, exchange(): return lax.all_to_all(values, axes, 0, 0, tiled=True)  77.1 us
    ppermute x1, starting transfers between devices, shards(): moved = lax.ppermute(normed.reshape(8, 64, 128), AXES, swapped)  7.08 us
    ppermute x1, starting transfers between devices, shards(): other = lax.ppermute(right, 'co', [(0, 1), (1, 0)])  5.88 us
    all_to_all x1, starting transfers between devices, exchange(): return lax.all_to_all(values, axes, 0, 0, tiled=True)  4.19 us
    pallas_call x1, Pallas kernels, make_edges(): pl.pallas_call(edges_kernel, out_shape=(jax.ShapeDtypeStruct((1024, 128),...  2.1 us
  transfers between devices with their start and end apart: 3, of which 2 were waited for; matrix products, arithmetic and copies ran while one was open for 0% of the time, Pallas kernels for 0%

profile of v5, /device:TPU:1, one launch (start us, length us, event | category | flops | bytes accessed | tf_op | source)
XLA Modules:
  0.0 101.1 jit_solution(10737578193797584585)
XLA Ops:
  0.0 2.1 %edges.1 = (bf16[1024,128]{1,0:T(8,128)(2,1)S(1)}, bf16[512,128]{1,0:T(8,128)(2,1)}, f32[2,128,128]{2,1,0:T(8,128)}) custom-call(bf16[8,64,128]{2,1,0:T(8,128)(2,1)} %pair_hbm.1, f32[1,128]{1,0:T(1,128)} %bitcast.13, f32[1,128]{1,0:T(1,128)} %bitcast.14, bf16[128,256]{1,0:T(8,128)(2,1)} %left_hbm.1, bf16[128,256]{1,0:T(8,128)(2,1)} %right_hbm.1, ...), custom_call_target="tpu_custom_call" | custom-call | tf_op jit(solution)/shard_map/edges/pallas_call | solution.py:106
  2.1 7.1 %collective-permute-start = (bf16[8,64,128]{2,1,0:T(8,128)(2,1)}, bf16[8,64,128]{2,1,0:T(8,128)(2,1)S(1)}, u32[]{:S(2)}, u32[]{:S(2)}) collective-permute-start(bf16[8,64,128]{2,1,0:T(8,128)(2,1)} %bitcast.17), channel_id=1, source_target_pairs={{0,3},{1,68},{2,129},{3,192},{4,260},{5,320},{6,389},{7,449},{8,11... | collective-permute-start | bytes 393224 | tf_op jit(solution)/shard_map/ppermute | solution.py:330
  9.2 35.7 %conditional.1 = (bf16[64,16,128]{2,1,0:T(8,128)(2,1)S(1)}) conditional(s32[]{:T(128)} %convert_element_type.3, bf16[64,16,128]{2,1,0:T(8,128)(2,1)S(1)} %bitcast.11, bf16[64,16,128]{2,1,0:T(8,128)(2,1)S(1)} %bitcast.12), branch_computations={%region_0.0_spmd, %region_1.0_spmd} | conditional | bytes 1048584 | solution.py:331
  9.2 35.6 %all_to_all.19 = bf16[64,16,128]{2,1,0:T(8,128)(2,1)S(1)} all-to-all(bf16[64,16,128]{2,1,0:T(8,128)(2,1)S(1)} %copy.13), channel_id=1, replica_groups=mesh['x'=4,'zh'=2,'y'=4,'co'=2,'n'=8] {'n','x','zh'}, dimensions={0} | all-to-all | bytes 524288 | tf_op jit(solution)/shard_map/cond/branch_1_fun/all_to_all | solution.py:306
  44.9 0.0 collective-permute-done.pair
  44.9 0.9 pack.1
  45.8 4.2 %all-to-all-start.1 = ((bf16[4,640,128]{2,1,0:T(8,128)(2,1)}), bf16[4,640,128]{2,1,0:T(8,128)(2,1)S(1)}, u32[]{:S(2)}, u32[]{:S(2)}) async-start(bf16[4,640,128]{2,1,0:T(8,128)(2,1)} %get-tuple-element.19), calls=%async_computation.1 | async-start | bytes 1310720 | tf_op jit(solution)/shard_map/all_to_all | solution.py:306
  50.0 0.0 copy-start.2
  50.0 5.9 %collective-permute-start.1 = (bf16[512,128]{1,0:T(8,128)(2,1)S(1)}, bf16[512,128]{1,0:T(8,128)(2,1)S(1)}, u32[]{:S(2)}, u32[]{:S(2)}) collective-permute-start(bf16[512,128]{1,0:T(8,128)(2,1)S(1)} %get-tuple-element.20.right), channel_id=1, source_target_pairs={{0,8},{8,0},{1,9},{9,1},{2,10},{10,2},{3,11},{11,3},{4,12},{12,4},... | collective-permute-start | bytes 393224 | tf_op jit(solution)/shard_map/ppermute | solution.py:339
  55.9 1.0 collective-permute-done.1.other
  56.9 0.8 all-to-all-done.1.received
  57.7 0.0 copy-done.2
  57.7 0.7 triangle.1
  58.3 0.0 copy-start.1
  58.3 0.0 copy-start.3
  58.4 22.2 %all_to_all.20.triangle = bf16[64,8,128]{2,1,0:T(8,128)(2,1)S(1)} all-to-all(bf16[64,8,128]{2,1,0:T(8,128)(2,1)S(1)} %bitcast.10), channel_id=1, replica_groups=mesh['x'=4,'zh'=2,'y'=4,'co'=2,'n'=8] {'n','x','zh'}, dimensions={0} | all-to-all | bytes 262144 | tf_op jit(solution)/shard_map/all_to_all | solution.py:306
  80.6 0.0 copy-start
  80.6 0.0 copy-done.1
  80.6 0.0 copy-done.3
  80.6 0.3 update.1
  80.9 19.3 %all_to_all.21.update = bf16[16,2,16,128]{3,2,1,0:T(8,128)(2,1)S(1)} all-to-all(bf16[16,2,16,128]{3,2,1,0:T(8,128)(2,1)S(1)} %bitcast.9), channel_id=1, replica_groups=mesh['x'=4,'zh'=2,'y'=4,'co'=2,'n'=8] {'co','n'}, dimensions={0} | all-to-all | bytes 262144 | tf_op jit(solution)/shard_map/all_to_all | solution.py:306
  100.2 0.0 copy-done
  100.2 0.9 order.1
  (1 shorter events, 0.0 us)
Async XLA Ops:
  2.1 42.8 %collective-permute-start = (bf16[8,64,128]{2,1,0:T(8,128)(2,1)}, bf16[8,64,128]{2,1,0:T(8,128)(2,1)S(1)}, u32[]{:S(2)}, u32[]{:S(2)}) collective-permute-start(bf16[8,64,128]{2,1,0:T(8,128)(2,1)} %bitcast.17), channel_id=1, source_target_pairs={{0,3},{1,68},{2,129},{3,192},{4,260},{5,320},{6,389},{7,449},{8,11... | collective-permute-start | bytes 393224 | tf_op jit(solution)/shard_map/ppermute | solution.py:330
  45.8 11.8 %all-to-all-start.1 = ((bf16[4,640,128]{2,1,0:T(8,128)(2,1)}), bf16[4,640,128]{2,1,0:T(8,128)(2,1)S(1)}, u32[]{:S(2)}, u32[]{:S(2)}) async-start(bf16[4,640,128]{2,1,0:T(8,128)(2,1)} %get-tuple-element.19), calls=%async_computation.1 | async-start | bytes 1310720 | tf_op jit(solution)/shard_map/all_to_all | solution.py:306
  50.0 7.6 %copy-start.2 = (bf16[128,128]{1,0:T(8,128)(2,1)S(1)}, bf16[128,128]{1,0:T(8,128)(2,1)}, u32[]{:S(2)}) copy-start(bf16[128,128]{1,0:T(8,128)(2,1)} %gate_weight.1) | copy-start | bytes 98308
  50.0 6.9 %collective-permute-start.1 = (bf16[512,128]{1,0:T(8,128)(2,1)S(1)}, bf16[512,128]{1,0:T(8,128)(2,1)S(1)}, u32[]{:S(2)}, u32[]{:S(2)}) collective-permute-start(bf16[512,128]{1,0:T(8,128)(2,1)S(1)} %get-tuple-element.20.right), channel_id=1, source_target_pairs={{0,8},{8,0},{1,9},{9,1},{2,10},{10,2},{3,11},{11,3},{4,12},{12,4},... | collective-permute-start | bytes 393224 | tf_op jit(solution)/shard_map/ppermute | solution.py:339
  58.3 22.2 %copy-start.1 = (f32[2,128,128]{2,1,0:T(8,128)S(1)}, f32[2,128,128]{2,1,0:T(8,128)}, u32[]{:S(2)}) copy-start(f32[2,128,128]{2,1,0:T(8,128)} %get-tuple-element.23.tall) | copy-start | bytes 393220
  58.3 22.2 %copy-start.3 = (bf16[128,128]{1,0:T(8,128)(2,1)S(1)}, bf16[128,128]{1,0:T(8,128)(2,1)}, u32[]{:S(2)}) copy-start(bf16[128,128]{1,0:T(8,128)(2,1)} %out_weight.1) | copy-start | bytes 98308
  80.6 19.6 %copy-start = (bf16[512,512]{1,0:T(8,128)(2,1)S(1)}, bf16[512,512]{1,0:T(8,128)(2,1)}, u32[]{:S(2)}) copy-start(bf16[512,512]{1,0:T(8,128)(2,1)} %constant.29.clone.matrix) | copy-start | bytes 1572868

commit v6 on v5

--- a/solution.py
+++ b/solution.py
@@ -96,7 +96,7 @@
             start = side * 8 + block * 2
             scratch[pl.ds(start, 64, stride=16), :] = even
             scratch[pl.ds(start + 1, 64, stride=16), :] = odd
-    edges[...] = scratch[...].astype(BF16)
+    edges[...] = scratch[:1024].astype(BF16)
     for result in results:
         result.wait()
 
@@ -124,7 +124,7 @@
             pltpu.VMEM((128, 256), BF16),
             row,
             row,
-            pltpu.VMEM((1024, 128), F32),
+            pltpu.VMEM((1024 + 16, 128), F32),
             pltpu.VMEM((512, 128), BF16),
             pltpu.VMEM((2, 128, 128), F32),
             pltpu.SemaphoreType.DMA((9,)),
@@ -184,7 +184,7 @@
         )
     lane_group = lax.broadcasted_iota(jnp.int32, (64, 128), 1) // 32
     for block in range(2):
-        rows[block] = total[:, block * 128 : block * 128 + 128]
+        rows[block, :256] = total[:, block * 128 : block * 128 + 128]
         taken = [rows[block, pl.ds(row, 64, stride=4), :] for row in range(4)]
         for group in range(4):
             turned = taken[0] if group == 0 else pltpu.roll(taken[0], 128 - group * 32, 1)
@@ -195,7 +195,7 @@
             turned = turned.astype(BF16).reshape(8, 8, 128)
             for target in range(8):
                 out[PLACES[target][block * 4 + group], target] = turned[target]
-    normed[...] = received[:, 512:].astype(F32).reshape(512, 128)
+    normed[:512] = received[:, 512:].astype(F32).reshape(512, 128)
     for part in range(4):
         first = part // 2 * 8 + part % 2 * 4
         pairs = jnp.concatenate(
@@ -216,7 +216,7 @@
         ),
         in_specs=[pl.BlockSpec(memory_space=pltpu.SMEM)]
         + [pl.BlockSpec(memory_space=pltpu.VMEM)] * 4,
-        scratch_shapes=[pltpu.VMEM((512, 128), F32), pltpu.VMEM((2, 256, 128), F32)],
+        scratch_shapes=[pltpu.VMEM((512 + 16, 128), F32), pltpu.VMEM((2, 256 + 8, 128), F32)],
         compiler_params=params(),
         name="triangle",
     )(place, received, right, other, gate_weight)
@@ -229,7 +229,7 @@
     center = (sums + pltpu.roll(sums, 4, 0)) / 128
     spread = (squares + pltpu.roll(squares, 4, 0)) / 128 - center * center
     scale = lax.rsqrt(spread + 1e-05)
-    scratch[...] = ((values - center) * scale).reshape(512, 128)
+    scratch[:512] = ((values - center) * scale).reshape(512, 128)
     for part in range(4):
         held = jnp.concatenate(
             [
@@ -250,7 +250,7 @@
     return pl.pallas_call(
         update_kernel,
         out_shape=jax.ShapeDtypeStruct((2, 8, 2, 16, 128), BF16),
-        scratch_shapes=[pltpu.VMEM((512, 128), F32)],
+        scratch_shapes=[pltpu.VMEM((512 + 8, 128), F32)],
         compiler_params=params(),
         name="update",
     )(triangle, gates, out_weight, tall)

time: 101 us -> 101 us (level)
  no operation moved by 1% of the time
where the time goes in v6:
time: 101 us
  blocking collectives  77.1 us (76%)
  starting transfers between devices  17.1 us (17%)
  Pallas kernels  4.91 us (5%)
  waiting for transfers between devices  1.74 us (2%)
    all_to_all x3, blocking collectives, exchange(): return lax.all_to_all(values, axes, 0, 0, tiled=True)  77.1 us
    ppermute x1, starting transfers between devices, shards(): moved = lax.ppermute(normed.reshape(8, 64, 128), AXES, swapped)  7.08 us
    ppermute x1, starting transfers between devices, shards(): other = lax.ppermute(right, 'co', [(0, 1), (1, 0)])  5.88 us
    all_to_all x1, starting transfers between devices, exchange(): return lax.all_to_all(values, axes, 0, 0, tiled=True)  4.19 us
    pallas_call x1, Pallas kernels, make_edges(): pl.pallas_call(edges_kernel, out_shape=(jax.ShapeDtypeStruct((1024, 128),...  2.1 us
  transfers between devices with their start and end apart: 3, of which 2 were waited for; matrix products, arithmetic and copies ran while one was open for 0% of the time, Pallas kernels for 0%

profile of v6, /device:TPU:1, one launch (start us, length us, event | category | flops | bytes accessed | tf_op | source)
XLA Modules:
  0.0 101.1 jit_solution(11121954838859161213)
XLA Ops:
  0.0 2.1 %edges.1 = (bf16[1024,128]{1,0:T(8,128)(2,1)S(1)}, bf16[512,128]{1,0:T(8,128)(2,1)}, f32[2,128,128]{2,1,0:T(8,128)}) custom-call(bf16[8,64,128]{2,1,0:T(8,128)(2,1)} %pair_hbm.1, f32[1,128]{1,0:T(1,128)} %bitcast.13, f32[1,128]{1,0:T(1,128)} %bitcast.14, bf16[128,256]{1,0:T(8,128)(2,1)} %left_hbm.1, bf16[128,256]{1,0:T(8,128)(2,1)} %right_hbm.1, ...), custom_call_target="tpu_custom_call" | custom-call | tf_op jit(solution)/shard_map/edges/pallas_call | solution.py:106
  2.1 7.1 %collective-permute-start = (bf16[8,64,128]{2,1,0:T(8,128)(2,1)}, bf16[8,64,128]{2,1,0:T(8,128)(2,1)S(1)}, u32[]{:S(2)}, u32[]{:S(2)}) collective-permute-start(bf16[8,64,128]{2,1,0:T(8,128)(2,1)} %bitcast.17), channel_id=1, source_target_pairs={{0,3},{1,68},{2,129},{3,192},{4,260},{5,320},{6,389},{7,449},{8,11... | collective-permute-start | bytes 393224 | tf_op jit(solution)/shard_map/ppermute | solution.py:330
  9.2 35.7 %conditional.1 = (bf16[64,16,128]{2,1,0:T(8,128)(2,1)S(1)}) conditional(s32[]{:T(128)} %convert_element_type.3, bf16[64,16,128]{2,1,0:T(8,128)(2,1)S(1)} %bitcast.11, bf16[64,16,128]{2,1,0:T(8,128)(2,1)S(1)} %bitcast.12), branch_computations={%region_0.0_spmd, %region_1.0_spmd} | conditional | bytes 1048584 | solution.py:331
  9.2 35.6 %all_to_all.19 = bf16[64,16,128]{2,1,0:T(8,128)(2,1)S(1)} all-to-all(bf16[64,16,128]{2,1,0:T(8,128)(2,1)S(1)} %copy.13), channel_id=1, replica_groups=mesh['x'=4,'zh'=2,'y'=4,'co'=2,'n'=8] {'n','x','zh'}, dimensions={0} | all-to-all | bytes 524288 | tf_op jit(solution)/shard_map/cond/branch_1_fun/all_to_all | solution.py:306
  44.9 0.0 collective-permute-done.pair
  44.9 0.9 pack.1
  45.8 4.2 %all-to-all-start.1 = ((bf16[4,640,128]{2,1,0:T(8,128)(2,1)}), bf16[4,640,128]{2,1,0:T(8,128)(2,1)S(1)}, u32[]{:S(2)}, u32[]{:S(2)}) async-start(bf16[4,640,128]{2,1,0:T(8,128)(2,1)} %get-tuple-element.19), calls=%async_computation.1 | async-start | bytes 1310720 | tf_op jit(solution)/shard_map/all_to_all | solution.py:306
  50.0 0.0 copy-start.2
  50.0 5.9 %collective-permute-start.1 = (bf16[512,128]{1,0:T(8,128)(2,1)S(1)}, bf16[512,128]{1,0:T(8,128)(2,1)S(1)}, u32[]{:S(2)}, u32[]{:S(2)}) collective-permute-start(bf16[512,128]{1,0:T(8,128)(2,1)S(1)} %get-tuple-element.20.right), channel_id=1, source_target_pairs={{0,8},{8,0},{1,9},{9,1},{2,10},{10,2},{3,11},{11,3},{4,12},{12,4},... | collective-permute-start | bytes 393224 | tf_op jit(solution)/shard_map/ppermute | solution.py:339
  55.9 1.0 collective-permute-done.1.other
  56.9 0.8 all-to-all-done.1.received
  57.7 0.0 copy-done.2
  57.7 0.7 triangle.1
  58.3 0.0 copy-start.1
  58.3 0.0 copy-start.3
  58.4 22.2 %all_to_all.20.triangle = bf16[64,8,128]{2,1,0:T(8,128)(2,1)S(1)} all-to-all(bf16[64,8,128]{2,1,0:T(8,128)(2,1)S(1)} %bitcast.10), channel_id=1, replica_groups=mesh['x'=4,'zh'=2,'y'=4,'co'=2,'n'=8] {'n','x','zh'}, dimensions={0} | all-to-all | bytes 262144 | tf_op jit(solution)/shard_map/all_to_all | solution.py:306
  80.6 0.0 copy-start
  80.6 0.0 copy-done.1
  80.6 0.0 copy-done.3
  80.6 0.3 update.1
  80.9 19.3 %all_to_all.21.update = bf16[16,2,16,128]{3,2,1,0:T(8,128)(2,1)S(1)} all-to-all(bf16[16,2,16,128]{3,2,1,0:T(8,128)(2,1)S(1)} %bitcast.9), channel_id=1, replica_groups=mesh['x'=4,'zh'=2,'y'=4,'co'=2,'n'=8] {'co','n'}, dimensions={0} | all-to-all | bytes 262144 | tf_op jit(solution)/shard_map/all_to_all | solution.py:306
  100.2 0.0 copy-done
  100.2 0.9 order.1
  (1 shorter events, 0.0 us)
Async XLA Ops:
  2.1 42.8 %collective-permute-start = (bf16[8,64,128]{2,1,0:T(8,128)(2,1)}, bf16[8,64,128]{2,1,0:T(8,128)(2,1)S(1)}, u32[]{:S(2)}, u32[]{:S(2)}) collective-permute-start(bf16[8,64,128]{2,1,0:T(8,128)(2,1)} %bitcast.17), channel_id=1, source_target_pairs={{0,3},{1,68},{2,129},{3,192},{4,260},{5,320},{6,389},{7,449},{8,11... | collective-permute-start | bytes 393224 | tf_op jit(solution)/shard_map/ppermute | solution.py:330
  45.8 11.8 %all-to-all-start.1 = ((bf16[4,640,128]{2,1,0:T(8,128)(2,1)}), bf16[4,640,128]{2,1,0:T(8,128)(2,1)S(1)}, u32[]{:S(2)}, u32[]{:S(2)}) async-start(bf16[4,640,128]{2,1,0:T(8,128)(2,1)} %get-tuple-element.19), calls=%async_computation.1 | async-start | bytes 1310720 | tf_op jit(solution)/shard_map/all_to_all | solution.py:306
  50.0 7.6 %copy-start.2 = (bf16[128,128]{1,0:T(8,128)(2,1)S(1)}, bf16[128,128]{1,0:T(8,128)(2,1)}, u32[]{:S(2)}) copy-start(bf16[128,128]{1,0:T(8,128)(2,1)} %gate_weight.1) | copy-start | bytes 98308
  50.0 6.9 %collective-permute-start.1 = (bf16[512,128]{1,0:T(8,128)(2,1)S(1)}, bf16[512,128]{1,0:T(8,128)(2,1)S(1)}, u32[]{:S(2)}, u32[]{:S(2)}) collective-permute-start(bf16[512,128]{1,0:T(8,128)(2,1)S(1)} %get-tuple-element.20.right), channel_id=1, source_target_pairs={{0,8},{8,0},{1,9},{9,1},{2,10},{10,2},{3,11},{11,3},{4,12},{12,4},... | collective-permute-start | bytes 393224 | tf_op jit(solution)/shard_map/ppermute | solution.py:339
  58.3 22.2 %copy-start.1 = (f32[2,128,128]{2,1,0:T(8,128)S(1)}, f32[2,128,128]{2,1,0:T(8,128)}, u32[]{:S(2)}) copy-start(f32[2,128,128]{2,1,0:T(8,128)} %get-tuple-element.23.tall) | copy-start | bytes 393220
  58.3 22.2 %copy-start.3 = (bf16[128,128]{1,0:T(8,128)(2,1)S(1)}, bf16[128,128]{1,0:T(8,128)(2,1)}, u32[]{:S(2)}) copy-start(bf16[128,128]{1,0:T(8,128)(2,1)} %out_weight.1) | copy-start | bytes 98308
  80.6 19.6 %copy-start = (bf16[512,512]{1,0:T(8,128)(2,1)S(1)}, bf16[512,512]{1,0:T(8,128)(2,1)}, u32[]{:S(2)}) copy-start(bf16[512,512]{1,0:T(8,128)(2,1)} %constant.29.clone.matrix) | copy-start | bytes 1572868

commit v7 on v6

--- a/solution.py
+++ b/solution.py
@@ -243,13 +243,13 @@
             out_weight[...], held, (((0,), (0,)), ((), ())), preferred_element_type=F32
         )
         update = (gates[part] * projected).astype(BF16)
-        out[part // 2, :, part % 2] = update.reshape(8, 16, 128)
+        out[:, part // 2, part % 2] = update.reshape(8, 16, 128)
 
 
 def make_update(triangle, gates, out_weight, tall):
     return pl.pallas_call(
         update_kernel,
-        out_shape=jax.ShapeDtypeStruct((2, 8, 2, 16, 128), BF16),
+        out_shape=jax.ShapeDtypeStruct((8, 2, 2, 16, 128), BF16),
         scratch_shapes=[pltpu.VMEM((512 + 8, 128), F32)],
         compiler_params=params(),
         name="update",
@@ -270,7 +270,7 @@
         ]
     pieces = [
         jnp.concatenate(
-            [update[core * 8 + held[block * 2 + side], half] for side in range(2) for core in range(2)],
+            [update[held[block * 2 + side] * 2 + core, half] for side in range(2) for core in range(2)],
             axis=1,
         )
         for block in range(4)
@@ -340,7 +340,7 @@
     triangle, gates = make_triangle(place, received, right, other, gate_weight)
     triangle = exchange(triangle.reshape(64, 8, 128), SPLIT)
     update = make_update(triangle, gates, out_weight, tall)
-    return make_order(place, exchange(update.reshape(16, 2, 16, 128), ("co", "n")))
+    return make_order(place, exchange(update.reshape(16, 2, 16, 128), ("n", "co")))
 
 
 def solution(mesh):

time: 101 us -> 101 us (level)
  no operation moved by 1% of the time
where the time goes in v7:
time: 101 us
  blocking collectives  76.7 us (76%)
  starting transfers between devices  17.1 us (17%)
  Pallas kernels  4.91 us (5%)
  waiting for transfers between devices  1.74 us (2%)
    all_to_all x3, blocking collectives, exchange(): return lax.all_to_all(values, axes, 0, 0, tiled=True)  76.7 us
    ppermute x1, starting transfers between devices, shards(): moved = lax.ppermute(normed.reshape(8, 64, 128), AXES, swapped)  7.08 us
    ppermute x1, starting transfers between devices, shards(): other = lax.ppermute(right, 'co', [(0, 1), (1, 0)])  5.88 us
    all_to_all x1, starting transfers between devices, exchange(): return lax.all_to_all(values, axes, 0, 0, tiled=True)  4.19 us
    pallas_call x1, Pallas kernels, make_edges(): pl.pallas_call(edges_kernel, out_shape=(jax.ShapeDtypeStruct((1024, 128),...  2.1 us
  transfers between devices with their start and end apart: 3, of which 2 were waited for; matrix products, arithmetic and copies ran while one was open for 0% of the time, Pallas kernels for 0%

profile of v7, /device:TPU:1, one launch (start us, length us, event | category | flops | bytes accessed | tf_op | source)
XLA Modules:
  0.0 100.6 jit_solution(4545294921297010979)
XLA Ops:
  0.0 2.1 %edges.1 = (bf16[1024,128]{1,0:T(8,128)(2,1)S(1)}, bf16[512,128]{1,0:T(8,128)(2,1)}, f32[2,128,128]{2,1,0:T(8,128)}) custom-call(bf16[8,64,128]{2,1,0:T(8,128)(2,1)} %pair_hbm.1, f32[1,128]{1,0:T(1,128)} %bitcast.13, f32[1,128]{1,0:T(1,128)} %bitcast.14, bf16[128,256]{1,0:T(8,128)(2,1)} %left_hbm.1, bf16[128,256]{1,0:T(8,128)(2,1)} %right_hbm.1, ...), custom_call_target="tpu_custom_call" | custom-call | tf_op jit(solution)/shard_map/edges/pallas_call | solution.py:106
  2.1 7.1 %collective-permute-start = (bf16[8,64,128]{2,1,0:T(8,128)(2,1)}, bf16[8,64,128]{2,1,0:T(8,128)(2,1)S(1)}, u32[]{:S(2)}, u32[]{:S(2)}) collective-permute-start(bf16[8,64,128]{2,1,0:T(8,128)(2,1)} %bitcast.17), channel_id=1, source_target_pairs={{0,3},{1,68},{2,129},{3,192},{4,260},{5,320},{6,389},{7,449},{8,11... | collective-permute-start | bytes 393224 | tf_op jit(solution)/shard_map/ppermute | solution.py:330
  9.2 35.7 %conditional.1 = (bf16[64,16,128]{2,1,0:T(8,128)(2,1)S(1)}) conditional(s32[]{:T(128)} %convert_element_type.3, bf16[64,16,128]{2,1,0:T(8,128)(2,1)S(1)} %bitcast.11, bf16[64,16,128]{2,1,0:T(8,128)(2,1)S(1)} %bitcast.12), branch_computations={%region_0.0_spmd, %region_1.0_spmd} | conditional | bytes 1048584 | solution.py:331
  9.2 35.6 %all_to_all.19 = bf16[64,16,128]{2,1,0:T(8,128)(2,1)S(1)} all-to-all(bf16[64,16,128]{2,1,0:T(8,128)(2,1)S(1)} %copy.13), channel_id=1, replica_groups=mesh['x'=4,'zh'=2,'y'=4,'co'=2,'n'=8] {'n','x','zh'}, dimensions={0} | all-to-all | bytes 524288 | tf_op jit(solution)/shard_map/cond/branch_1_fun/all_to_all | solution.py:306
  44.9 0.0 collective-permute-done.pair
  44.9 0.9 pack.1
  45.8 4.2 %all-to-all-start.1 = ((bf16[4,640,128]{2,1,0:T(8,128)(2,1)}), bf16[4,640,128]{2,1,0:T(8,128)(2,1)S(1)}, u32[]{:S(2)}, u32[]{:S(2)}) async-start(bf16[4,640,128]{2,1,0:T(8,128)(2,1)} %get-tuple-element.19), calls=%async_computation.1 | async-start | bytes 1310720 | tf_op jit(solution)/shard_map/all_to_all | solution.py:306
  50.0 0.0 copy-start.2
  50.0 5.9 %collective-permute-start.1 = (bf16[512,128]{1,0:T(8,128)(2,1)S(1)}, bf16[512,128]{1,0:T(8,128)(2,1)S(1)}, u32[]{:S(2)}, u32[]{:S(2)}) collective-permute-start(bf16[512,128]{1,0:T(8,128)(2,1)S(1)} %get-tuple-element.20.right), channel_id=1, source_target_pairs={{0,8},{8,0},{1,9},{9,1},{2,10},{10,2},{3,11},{11,3},{4,12},{12,4},... | collective-permute-start | bytes 393224 | tf_op jit(solution)/shard_map/ppermute | solution.py:339
  55.9 1.0 collective-permute-done.1.other
  56.9 0.8 all-to-all-done.1.received
  57.7 0.0 copy-done.2
  57.7 0.7 triangle.1
  58.3 0.0 copy-start.1
  58.3 0.0 copy-start.3
  58.4 22.2 %all_to_all.20.triangle = bf16[64,8,128]{2,1,0:T(8,128)(2,1)S(1)} all-to-all(bf16[64,8,128]{2,1,0:T(8,128)(2,1)S(1)} %bitcast.10), channel_id=1, replica_groups=mesh['x'=4,'zh'=2,'y'=4,'co'=2,'n'=8] {'n','x','zh'}, dimensions={0} | all-to-all | bytes 262144 | tf_op jit(solution)/shard_map/all_to_all | solution.py:306
  80.6 0.0 copy-start
  80.6 0.0 copy-done.1
  80.6 0.0 copy-done.3
  80.6 0.3 update.1
  80.9 18.8 %all_to_all.21.update = bf16[16,2,16,128]{3,2,1,0:T(8,128)(2,1)S(1)} all-to-all(bf16[16,2,16,128]{3,2,1,0:T(8,128)(2,1)S(1)} %bitcast.9), channel_id=1, replica_groups=mesh['x'=4,'zh'=2,'y'=4,'co'=2,'n'=8] {'n','co'}, dimensions={0} | all-to-all | bytes 262144 | tf_op jit(solution)/shard_map/all_to_all | solution.py:306
  99.7 0.0 copy-done
  99.7 0.9 order.1
  (1 shorter events, 0.0 us)
Async XLA Ops:
  2.1 42.8 %collective-permute-start = (bf16[8,64,128]{2,1,0:T(8,128)(2,1)}, bf16[8,64,128]{2,1,0:T(8,128)(2,1)S(1)}, u32[]{:S(2)}, u32[]{:S(2)}) collective-permute-start(bf16[8,64,128]{2,1,0:T(8,128)(2,1)} %bitcast.17), channel_id=1, source_target_pairs={{0,3},{1,68},{2,129},{3,192},{4,260},{5,320},{6,389},{7,449},{8,11... | collective-permute-start | bytes 393224 | tf_op jit(solution)/shard_map/ppermute | solution.py:330
  45.8 11.8 %all-to-all-start.1 = ((bf16[4,640,128]{2,1,0:T(8,128)(2,1)}), bf16[4,640,128]{2,1,0:T(8,128)(2,1)S(1)}, u32[]{:S(2)}, u32[]{:S(2)}) async-start(bf16[4,640,128]{2,1,0:T(8,128)(2,1)} %get-tuple-element.19), calls=%async_computation.1 | async-start | bytes 1310720 | tf_op jit(solution)/shard_map/all_to_all | solution.py:306
  50.0 7.6 %copy-start.2 = (bf16[128,128]{1,0:T(8,128)(2,1)S(1)}, bf16[128,128]{1,0:T(8,128)(2,1)}, u32[]{:S(2)}) copy-start(bf16[128,128]{1,0:T(8,128)(2,1)} %gate_weight.1) | copy-start | bytes 98308
  50.0 6.9 %collective-permute-start.1 = (bf16[512,128]{1,0:T(8,128)(2,1)S(1)}, bf16[512,128]{1,0:T(8,128)(2,1)S(1)}, u32[]{:S(2)}, u32[]{:S(2)}) collective-permute-start(bf16[512,128]{1,0:T(8,128)(2,1)S(1)} %get-tuple-element.20.right), channel_id=1, source_target_pairs={{0,8},{8,0},{1,9},{9,1},{2,10},{10,2},{3,11},{11,3},{4,12},{12,4},... | collective-permute-start | bytes 393224 | tf_op jit(solution)/shard_map/ppermute | solution.py:339
  58.3 22.2 %copy-start.1 = (f32[2,128,128]{2,1,0:T(8,128)S(1)}, f32[2,128,128]{2,1,0:T(8,128)}, u32[]{:S(2)}) copy-start(f32[2,128,128]{2,1,0:T(8,128)} %get-tuple-element.23.tall) | copy-start | bytes 393220
  58.3 22.2 %copy-start.3 = (bf16[128,128]{1,0:T(8,128)(2,1)S(1)}, bf16[128,128]{1,0:T(8,128)(2,1)}, u32[]{:S(2)}) copy-start(bf16[128,128]{1,0:T(8,128)(2,1)} %out_weight.1) | copy-start | bytes 98308
  80.6 19.2 %copy-start = (bf16[512,512]{1,0:T(8,128)(2,1)S(1)}, bf16[512,512]{1,0:T(8,128)(2,1)}, u32[]{:S(2)}) copy-start(bf16[512,512]{1,0:T(8,128)(2,1)} %constant.29.clone.matrix) | copy-start | bytes 1572868

commit v8 on v7

--- a/solution.py
+++ b/solution.py
@@ -142,21 +142,17 @@
     )
 
 
-def pack_kernel(edges, pair, payload, right):
+def pack_kernel(edges, pair, payload):
     left = edges[:, :8].reshape(512, 128)
     for target in range(4):
         payload[target, :512] = left
         payload[target, 512:] = pair[:, target * 16 : target * 16 + 16].reshape(128, 128)
-    right[...] = edges[:, 8:].reshape(512, 128)
 
 
 def make_pack(edges, pair):
     return pl.pallas_call(
         pack_kernel,
-        out_shape=(
-            jax.ShapeDtypeStruct((4, 640, 128), BF16),
-            jax.ShapeDtypeStruct((512, 128), BF16),
-        ),
+        out_shape=jax.ShapeDtypeStruct((4, 640, 128), BF16),
         compiler_params=params(),
         name="pack",
     )(edges, pair)
@@ -334,8 +330,8 @@
         lambda held: held,
         edges.reshape(64, 16, 128),
     )
-    payload, right = make_pack(edges, moved)
-    received = exchange(payload, "y")
+    received = exchange(make_pack(edges, moved), "y")
+    right = edges[:, 8:].reshape(512, 128)
     other = lax.ppermute(right, "co", [(0, 1), (1, 0)])
     triangle, gates = make_triangle(place, received, right, other, gate_weight)
     triangle = exchange(triangle.reshape(64, 8, 128), SPLIT)

time: 101 us -> 101 us (level)
  no operation moved by 1% of the time
where the time goes in v8:
time: 101 us
  blocking collectives  76.7 us (76%)
  starting transfers between devices  17 us (17%)
  Pallas kernels  4.89 us (5%)
  waiting for transfers between devices  1.84 us (2%)
    all_to_all x3, blocking collectives, exchange(): return lax.all_to_all(values, axes, 0, 0, tiled=True)  76.7 us
    ppermute x1, starting transfers between devices, shards(): moved = lax.ppermute(normed.reshape(8, 64, 128), AXES, swapped)  7.08 us
    ppermute x1, starting transfers between devices, shards(): other = lax.ppermute(right, 'co', [(0, 1), (1, 0)])  5.76 us
    all_to_all x1, starting transfers between devices, exchange(): return lax.all_to_all(values, axes, 0, 0, tiled=True)  4.19 us
    pallas_call x1, Pallas kernels, make_edges(): pl.pallas_call(edges_kernel, out_shape=(jax.ShapeDtypeStruct((1024, 128),...  2.11 us
  transfers between devices with their start and end apart: 3, of which 2 were waited for; matrix products, arithmetic and copies ran while one was open for 0% of the time, Pallas kernels for 0%

profile of v8, /device:TPU:1, one launch (start us, length us, event | category | flops | bytes accessed | tf_op | source)
XLA Modules:
  0.0 100.6 jit_solution(13898755075680074945)
XLA Ops:
  0.0 2.1 %edges.1 = (bf16[1024,128]{1,0:T(8,128)(2,1)S(1)}, bf16[512,128]{1,0:T(8,128)(2,1)}, f32[2,128,128]{2,1,0:T(8,128)}) custom-call(bf16[8,64,128]{2,1,0:T(8,128)(2,1)} %pair_hbm.1, f32[1,128]{1,0:T(1,128)} %bitcast.15, f32[1,128]{1,0:T(1,128)} %bitcast.16, bf16[128,256]{1,0:T(8,128)(2,1)} %left_hbm.1, bf16[128,256]{1,0:T(8,128)(2,1)} %right_hbm.1, ...), custom_call_target="tpu_custom_call" | custom-call | tf_op jit(solution)/shard_map/edges/pallas_call | solution.py:106
  2.1 7.1 %collective-permute-start = (bf16[8,64,128]{2,1,0:T(8,128)(2,1)}, bf16[8,64,128]{2,1,0:T(8,128)(2,1)S(1)}, u32[]{:S(2)}, u32[]{:S(2)}) collective-permute-start(bf16[8,64,128]{2,1,0:T(8,128)(2,1)} %bitcast.19), channel_id=1, source_target_pairs={{0,3},{1,68},{2,129},{3,192},{4,260},{5,320},{6,389},{7,449},{8,11... | collective-permute-start | bytes 393224 | tf_op jit(solution)/shard_map/ppermute | solution.py:326
  9.2 35.7 %conditional.1 = (bf16[64,16,128]{2,1,0:T(8,128)(2,1)S(1)}) conditional(s32[]{:T(128)} %convert_element_type.3, bf16[64,16,128]{2,1,0:T(8,128)(2,1)S(1)} %bitcast.13, bf16[64,16,128]{2,1,0:T(8,128)(2,1)S(1)} %bitcast.14), branch_computations={%region_0.0_spmd, %region_1.0_spmd} | conditional | bytes 1048584 | solution.py:327
  9.2 35.6 %all_to_all.19 = bf16[64,16,128]{2,1,0:T(8,128)(2,1)S(1)} all-to-all(bf16[64,16,128]{2,1,0:T(8,128)(2,1)S(1)} %copy.13), channel_id=1, replica_groups=mesh['x'=4,'zh'=2,'y'=4,'co'=2,'n'=8] {'n','x','zh'}, dimensions={0} | all-to-all | bytes 524288 | tf_op jit(solution)/shard_map/cond/branch_1_fun/all_to_all | solution.py:302
  44.9 0.0 collective-permute-done.pair
  44.9 0.9 pack.1
  45.8 4.2 %all-to-all-start.1 = ((bf16[4,640,128]{2,1,0:T(8,128)(2,1)}), bf16[4,640,128]{2,1,0:T(8,128)(2,1)S(1)}, u32[]{:S(2)}, u32[]{:S(2)}) async-start(bf16[4,640,128]{2,1,0:T(8,128)(2,1)} %pack.1), calls=%async_computation.1 | async-start | bytes 1310720 | tf_op jit(solution)/shard_map/all_to_all | solution.py:302
  50.0 0.0 copy-start.2
  50.0 5.8 %collective-permute-start.1 = (bf16[512,128]{1,0:T(8,128)(2,1)S(1)}, bf16[512,128]{1,0:T(8,128)(2,1)S(1)}, u32[]{:S(2)}, u32[]{:S(2)}) collective-permute-start(bf16[512,128]{1,0:T(8,128)(2,1)S(1)} %slice_bitcast_fusion.right), channel_id=1, source_target_pairs={{0,8},{8,0},{1,9},{9,1},{2,10},{10,2},{3,11},{11,3},{4,12},{12,4},... | collective-permute-start | bytes 393224 | tf_op jit(solution)/shard_map/ppermute | solution.py:335
  55.8 1.0 collective-permute-done.1.other
  56.8 0.9 all-to-all-done.1.received
  57.6 0.0 copy-done.2
  57.6 0.7 triangle.1
  58.3 0.0 copy-start.1
  58.3 0.0 copy-start.3
  58.3 22.2 %all_to_all.20.triangle = bf16[64,8,128]{2,1,0:T(8,128)(2,1)S(1)} all-to-all(bf16[64,8,128]{2,1,0:T(8,128)(2,1)S(1)} %bitcast.12), channel_id=1, replica_groups=mesh['x'=4,'zh'=2,'y'=4,'co'=2,'n'=8] {'n','x','zh'}, dimensions={0} | all-to-all | bytes 262144 | tf_op jit(solution)/shard_map/all_to_all | solution.py:302
  80.6 0.0 copy-start
  80.6 0.0 copy-done.1
  80.6 0.0 copy-done.3
  80.6 0.3 update.1
  80.9 18.8 %all_to_all.21.update = bf16[16,2,16,128]{3,2,1,0:T(8,128)(2,1)S(1)} all-to-all(bf16[16,2,16,128]{3,2,1,0:T(8,128)(2,1)S(1)} %bitcast.11), channel_id=1, replica_groups=mesh['x'=4,'zh'=2,'y'=4,'co'=2,'n'=8] {'n','co'}, dimensions={0} | all-to-all | bytes 262144 | tf_op jit(solution)/shard_map/all_to_all | solution.py:302
  99.7 0.0 copy-done
  99.7 0.9 order.1
  (2 shorter events, 0.0 us)
Async XLA Ops:
  2.1 42.8 %collective-permute-start = (bf16[8,64,128]{2,1,0:T(8,128)(2,1)}, bf16[8,64,128]{2,1,0:T(8,128)(2,1)S(1)}, u32[]{:S(2)}, u32[]{:S(2)}) collective-permute-start(bf16[8,64,128]{2,1,0:T(8,128)(2,1)} %bitcast.19), channel_id=1, source_target_pairs={{0,3},{1,68},{2,129},{3,192},{4,260},{5,320},{6,389},{7,449},{8,11... | collective-permute-start | bytes 393224 | tf_op jit(solution)/shard_map/ppermute | solution.py:326
  45.8 11.8 %all-to-all-start.1 = ((bf16[4,640,128]{2,1,0:T(8,128)(2,1)}), bf16[4,640,128]{2,1,0:T(8,128)(2,1)S(1)}, u32[]{:S(2)}, u32[]{:S(2)}) async-start(bf16[4,640,128]{2,1,0:T(8,128)(2,1)} %pack.1), calls=%async_computation.1 | async-start | bytes 1310720 | tf_op jit(solution)/shard_map/all_to_all | solution.py:302
  50.0 7.6 %copy-start.2 = (bf16[128,128]{1,0:T(8,128)(2,1)S(1)}, bf16[128,128]{1,0:T(8,128)(2,1)}, u32[]{:S(2)}) copy-start(bf16[128,128]{1,0:T(8,128)(2,1)} %gate_weight.1) | copy-start | bytes 98308
  50.0 6.7 %collective-permute-start.1 = (bf16[512,128]{1,0:T(8,128)(2,1)S(1)}, bf16[512,128]{1,0:T(8,128)(2,1)S(1)}, u32[]{:S(2)}, u32[]{:S(2)}) collective-permute-start(bf16[512,128]{1,0:T(8,128)(2,1)S(1)} %slice_bitcast_fusion.right), channel_id=1, source_target_pairs={{0,8},{8,0},{1,9},{9,1},{2,10},{10,2},{3,11},{11,3},{4,12},{12,4},... | collective-permute-start | bytes 393224 | tf_op jit(solution)/shard_map/ppermute | solution.py:335
  58.3 22.3 %copy-start.1 = (f32[2,128,128]{2,1,0:T(8,128)S(1)}, f32[2,128,128]{2,1,0:T(8,128)}, u32[]{:S(2)}) copy-start(f32[2,128,128]{2,1,0:T(8,128)} %get-tuple-element.25.tall) | copy-start | bytes 393220
  58.3 22.2 %copy-start.3 = (bf16[128,128]{1,0:T(8,128)(2,1)S(1)}, bf16[128,128]{1,0:T(8,128)(2,1)}, u32[]{:S(2)}) copy-start(bf16[128,128]{1,0:T(8,128)(2,1)} %out_weight.1) | copy-start | bytes 98308
  80.6 19.2 %copy-start = (bf16[512,512]{1,0:T(8,128)(2,1)S(1)}, bf16[512,512]{1,0:T(8,128)(2,1)}, u32[]{:S(2)}) copy-start(bf16[512,512]{1,0:T(8,128)(2,1)} %constant.29.clone.matrix) | copy-start | bytes 1572868

commit v9 on v8

--- a/solution.py
+++ b/solution.py
@@ -89,7 +89,7 @@
         both = lax.dot_general(
             weight[...], rounded, (((0,), (1,)), ((), ())), preferred_element_type=F32
         )
-        edge = jax.nn.sigmoid(both[128:]) * both[:128]
+        edge = (0.5 * jnp.tanh(0.5 * both[128:]) + 0.5) * both[:128]
         for block in range(4):
             lanes = slice(block * 128, block * 128 + 128)
             even, odd = cross_halves(edge[:64, lanes], edge[64:, lanes])

time: 101 us -> 101 us (level)
  no operation moved by 1% of the time
where the time goes in v9:
time: 101 us
  blocking collectives  76.7 us (76%)
  starting transfers between devices  17 us (17%)
  Pallas kernels  4.91 us (5%)
  waiting for transfers between devices  1.84 us (2%)
    all_to_all x3, blocking collectives, exchange(): return lax.all_to_all(values, axes, 0, 0, tiled=True)  76.7 us
    ppermute x1, starting transfers between devices, shards(): moved = lax.ppermute(normed.reshape(8, 64, 128), AXES, swapped)  7.08 us
    ppermute x1, starting transfers between devices, shards(): other = lax.ppermute(right, 'co', [(0, 1), (1, 0)])  5.76 us
    all_to_all x1, starting transfers between devices, exchange(): return lax.all_to_all(values, axes, 0, 0, tiled=True)  4.18 us
    pallas_call x1, Pallas kernels, make_edges(): pl.pallas_call(edges_kernel, out_shape=(jax.ShapeDtypeStruct((1024, 128),...  2.12 us
  transfers between devices with their start and end apart: 3, of which 2 were waited for; matrix products, arithmetic and copies ran while one was open for 0% of the time, Pallas kernels for 0%

profile of v9, /device:TPU:1, one launch (start us, length us, event | category | flops | bytes accessed | tf_op | source)
XLA Modules:
  0.0 100.6 jit_solution(12092106489350736568)
XLA Ops:
  0.0 2.1 %edges.1 = (bf16[1024,128]{1,0:T(8,128)(2,1)S(1)}, bf16[512,128]{1,0:T(8,128)(2,1)}, f32[2,128,128]{2,1,0:T(8,128)}) custom-call(bf16[8,64,128]{2,1,0:T(8,128)(2,1)} %pair_hbm.1, f32[1,128]{1,0:T(1,128)} %bitcast.15, f32[1,128]{1,0:T(1,128)} %bitcast.16, bf16[128,256]{1,0:T(8,128)(2,1)} %left_hbm.1, bf16[128,256]{1,0:T(8,128)(2,1)} %right_hbm.1, ...), custom_call_target="tpu_custom_call" | custom-call | tf_op jit(solution)/shard_map/edges/pallas_call | solution.py:106
  2.1 7.1 %collective-permute-start = (bf16[8,64,128]{2,1,0:T(8,128)(2,1)}, bf16[8,64,128]{2,1,0:T(8,128)(2,1)S(1)}, u32[]{:S(2)}, u32[]{:S(2)}) collective-permute-start(bf16[8,64,128]{2,1,0:T(8,128)(2,1)} %bitcast.19), channel_id=1, source_target_pairs={{0,3},{1,68},{2,129},{3,192},{4,260},{5,320},{6,389},{7,449},{8,11... | collective-permute-start | bytes 393224 | tf_op jit(solution)/shard_map/ppermute | solution.py:326
  9.2 35.7 %conditional.1 = (bf16[64,16,128]{2,1,0:T(8,128)(2,1)S(1)}) conditional(s32[]{:T(128)} %convert_element_type.3, bf16[64,16,128]{2,1,0:T(8,128)(2,1)S(1)} %bitcast.13, bf16[64,16,128]{2,1,0:T(8,128)(2,1)S(1)} %bitcast.14), branch_computations={%region_0.0_spmd, %region_1.0_spmd} | conditional | bytes 1048584 | solution.py:327
  9.3 35.7 %all_to_all.19 = bf16[64,16,128]{2,1,0:T(8,128)(2,1)S(1)} all-to-all(bf16[64,16,128]{2,1,0:T(8,128)(2,1)S(1)} %copy.13), channel_id=1, replica_groups=mesh['x'=4,'zh'=2,'y'=4,'co'=2,'n'=8] {'n','x','zh'}, dimensions={0} | all-to-all | bytes 524288 | tf_op jit(solution)/shard_map/cond/branch_1_fun/all_to_all | solution.py:302
  44.9 0.0 collective-permute-done.pair
  44.9 0.9 pack.1
  45.8 4.2 %all-to-all-start.1 = ((bf16[4,640,128]{2,1,0:T(8,128)(2,1)}), bf16[4,640,128]{2,1,0:T(8,128)(2,1)S(1)}, u32[]{:S(2)}, u32[]{:S(2)}) async-start(bf16[4,640,128]{2,1,0:T(8,128)(2,1)} %pack.1), calls=%async_computation.1 | async-start | bytes 1310720 | tf_op jit(solution)/shard_map/all_to_all | solution.py:302
  50.0 0.0 copy-start.2
  50.0 5.8 %collective-permute-start.1 = (bf16[512,128]{1,0:T(8,128)(2,1)S(1)}, bf16[512,128]{1,0:T(8,128)(2,1)S(1)}, u32[]{:S(2)}, u32[]{:S(2)}) collective-permute-start(bf16[512,128]{1,0:T(8,128)(2,1)S(1)} %slice_bitcast_fusion.right), channel_id=1, source_target_pairs={{0,8},{8,0},{1,9},{9,1},{2,10},{10,2},{3,11},{11,3},{4,12},{12,4},... | collective-permute-start | bytes 393224 | tf_op jit(solution)/shard_map/ppermute | solution.py:335
  55.8 1.0 collective-permute-done.1.other
  56.8 0.9 all-to-all-done.1.received
  57.7 0.0 copy-done.2
  57.7 0.7 triangle.1
  58.3 0.0 copy-start.1
  58.3 0.0 copy-start.3
  58.4 22.2 %all_to_all.20.triangle = bf16[64,8,128]{2,1,0:T(8,128)(2,1)S(1)} all-to-all(bf16[64,8,128]{2,1,0:T(8,128)(2,1)S(1)} %bitcast.12), channel_id=1, replica_groups=mesh['x'=4,'zh'=2,'y'=4,'co'=2,'n'=8] {'n','x','zh'}, dimensions={0} | all-to-all | bytes 262144 | tf_op jit(solution)/shard_map/all_to_all | solution.py:302
  80.6 0.0 copy-start
  80.6 0.0 copy-done.1
  80.6 0.0 copy-done.3
  80.6 0.3 update.1
  80.9 18.8 %all_to_all.21.update = bf16[16,2,16,128]{3,2,1,0:T(8,128)(2,1)S(1)} all-to-all(bf16[16,2,16,128]{3,2,1,0:T(8,128)(2,1)S(1)} %bitcast.11), channel_id=1, replica_groups=mesh['x'=4,'zh'=2,'y'=4,'co'=2,'n'=8] {'n','co'}, dimensions={0} | all-to-all | bytes 262144 | tf_op jit(solution)/shard_map/all_to_all | solution.py:302
  99.7 0.0 copy-done
  99.7 0.9 order.1
  (2 shorter events, 0.0 us)
Async XLA Ops:
  2.1 42.8 %collective-permute-start = (bf16[8,64,128]{2,1,0:T(8,128)(2,1)}, bf16[8,64,128]{2,1,0:T(8,128)(2,1)S(1)}, u32[]{:S(2)}, u32[]{:S(2)}) collective-permute-start(bf16[8,64,128]{2,1,0:T(8,128)(2,1)} %bitcast.19), channel_id=1, source_target_pairs={{0,3},{1,68},{2,129},{3,192},{4,260},{5,320},{6,389},{7,449},{8,11... | collective-permute-start | bytes 393224 | tf_op jit(solution)/shard_map/ppermute | solution.py:326
  45.8 11.8 %all-to-all-start.1 = ((bf16[4,640,128]{2,1,0:T(8,128)(2,1)}), bf16[4,640,128]{2,1,0:T(8,128)(2,1)S(1)}, u32[]{:S(2)}, u32[]{:S(2)}) async-start(bf16[4,640,128]{2,1,0:T(8,128)(2,1)} %pack.1), calls=%async_computation.1 | async-start | bytes 1310720 | tf_op jit(solution)/shard_map/all_to_all | solution.py:302
  50.0 7.6 %copy-start.2 = (bf16[128,128]{1,0:T(8,128)(2,1)S(1)}, bf16[128,128]{1,0:T(8,128)(2,1)}, u32[]{:S(2)}) copy-start(bf16[128,128]{1,0:T(8,128)(2,1)} %gate_weight.1) | copy-start | bytes 98308
  50.0 6.7 %collective-permute-start.1 = (bf16[512,128]{1,0:T(8,128)(2,1)S(1)}, bf16[512,128]{1,0:T(8,128)(2,1)S(1)}, u32[]{:S(2)}, u32[]{:S(2)}) collective-permute-start(bf16[512,128]{1,0:T(8,128)(2,1)S(1)} %slice_bitcast_fusion.right), channel_id=1, source_target_pairs={{0,8},{8,0},{1,9},{9,1},{2,10},{10,2},{3,11},{11,3},{4,12},{12,4},... | collective-permute-start | bytes 393224 | tf_op jit(solution)/shard_map/ppermute | solution.py:335
  58.3 22.2 %copy-start.1 = (f32[2,128,128]{2,1,0:T(8,128)S(1)}, f32[2,128,128]{2,1,0:T(8,128)}, u32[]{:S(2)}) copy-start(f32[2,128,128]{2,1,0:T(8,128)} %get-tuple-element.25.tall) | copy-start | bytes 393220
  58.3 22.2 %copy-start.3 = (bf16[128,128]{1,0:T(8,128)(2,1)S(1)}, bf16[128,128]{1,0:T(8,128)(2,1)}, u32[]{:S(2)}) copy-start(bf16[128,128]{1,0:T(8,128)(2,1)} %out_weight.1) | copy-start | bytes 98308
  80.6 19.2 %copy-start = (bf16[512,512]{1,0:T(8,128)(2,1)S(1)}, bf16[512,512]{1,0:T(8,128)(2,1)}, u32[]{:S(2)}) copy-start(bf16[512,512]{1,0:T(8,128)(2,1)} %constant.29.clone.matrix) | copy-start | bytes 1572868
